TPU v7x, 512 devices: a whole 4x8x8 slice. The times are simulated.
512 devices in a mesh: seq: 64 (over z, x, y_lo), fsdp: 8 (over y_hi, core).
Axes of the slice: x: 4, y: 8 (y_hi: 4, y_lo: 2; y = y_hi * 2 + y_lo), z: 8, core: 2. Of those that a mesh axis runs over, the one named last changes fastest.
Arguments:
- queries: bfloat16 [8192, 1024], P('seq', 'fsdp'), may hold values from -8 to 8
- keys: bfloat16 [8192, 1024], P('seq', 'fsdp'), may hold values from -8 to 8
- values: bfloat16 [8192, 1024], P('seq', 'fsdp'), may hold values from -12 to 12
- residual: bfloat16 [8192, 3072], P('seq', 'fsdp'), may hold values from -6 to 6
- gate: float32 [3072], replicated, may hold values from 0.25 to 2
- w_out: bfloat16 [1024, 3072], P('fsdp', 'seq'), may hold values from -0.1875 to 0.1875
- grad_out: bfloat16 [8192, 3072], P('seq'), may hold values from -6 to 6
- group_mask: int32 [128, 128], replicated, may hold values from 0 to 1, as said below
- group_of_slot: int32 [128], replicated, may hold values from 0 to 127, each once
Outputs:
- layer_out: bfloat16 [8192, 3072], P('seq', 'fsdp')
- d_queries: bfloat16 [8192, 1024], P('seq', 'fsdp')
- d_keys: bfloat16 [8192, 1024], P('seq', 'fsdp')
- d_values: bfloat16 [8192, 1024], P('seq', 'fsdp')
- d_weight: float32 [1024, 3072], P('fsdp', 'seq')
Inputs may be any that keep to these rules, and one draw needn't show every extreme that they name: group_mask[i, j] is 1 where j equals i and 0 where j exceeds i. `group_of_slot`: each group stands in exactly one slot.
All inputs are finite; a program needn't handle non-finite values.
Results may differ from a plain program's by a relative error of at most 0.035.
Values may be sent and summed in bfloat16 or wider, within the bound.
No kernel may reach another device: no remote copies, remote signals or barrier semaphores. Data moves between devices by JAX's collectives and lax.ppermute only.
A program may use at most 64 MiB of HBM per device.

v0:
```python
import math

import jax
import jax.numpy as jnp
from jax import lax
from jax.sharding import PartitionSpec as P

HD = 64
GROUP = 64


def expand(group_table):
    rows_n, cols_n = group_table.shape
    grown = jnp.broadcast_to(group_table[:, None, :, None], (rows_n, GROUP, cols_n, GROUP))
    return grown.reshape(rows_n * GROUP, cols_n * GROUP) == 1


def local(queries, keys, values, residual, gate, w_out, grad_out, group_mask, group_of_slot):
    tok_rows = queries.shape[0]
    feature_count = queries.shape[1]
    heads_here = feature_count // HD
    score_scale = HD ** (-0.5)
    slot_count = group_of_slot.shape[0]
    local_count = tok_rows // GROUP
    per_block = math.gcd(slot_count, max(1, 512 // GROUP))
    block_rows = per_block * GROUP
    block_count = slot_count // per_block
    seq_place = lax.axis_index("seq")
    local_groups = lax.dynamic_slice_in_dim(group_of_slot, seq_place * local_count, local_count, 0)
    row_table = jnp.take(group_mask, local_groups, axis=0)
    seen_by_local = jnp.take(row_table, group_of_slot, axis=1)
    col_table = jnp.take(group_mask, local_groups, axis=1)
    seeing_local = jnp.take(col_table, group_of_slot, axis=0)
    query_heads = queries.reshape(tok_rows, heads_here, HD)
    key_all, value_all = (
        lax.all_gather(keys, "seq", axis=0, tiled=True),
        lax.all_gather(values, "seq", axis=0, tiled=True),
    )
    key_groups = key_all.reshape(slot_count, GROUP, heads_here, HD)
    value_groups = value_all.reshape(slot_count, GROUP, heads_here, HD)
    needed = jnp.ones((block_count,), jnp.bool_)
    key_blocks = key_groups.reshape(block_count, block_rows, heads_here, HD)
    value_blocks = value_groups.reshape(block_count, block_rows, heads_here, HD)
    seen_blocks = seen_by_local.reshape(local_count, block_count, per_block).transpose(1, 0, 2)

    def masked_scores(query_part, key_part, seen_mask):
        raw_scores = (
            jnp.einsum("qhd,khd->hqk", query_part, key_part, preferred_element_type=jnp.float32)
            * score_scale
        )
        return jnp.where(expand(seen_mask)[None], raw_scores, -jnp.inf)

    def stat_step(totals, block_item):
        key_block, seen_mask, block_needed = block_item
        row_top, exp_total = totals
        scores = masked_scores(query_heads, key_block, seen_mask)
        new_top = jnp.maximum(row_top, jnp.max(scores, axis=2))
        safe_top = jnp.where(jnp.isfinite(new_top), new_top, 0.0)
        exp_total = exp_total * jnp.exp(row_top - safe_top) + jnp.sum(
            jnp.exp(scores - safe_top[..., None]), axis=2
        )
        return ((new_top, exp_total), None)

    start_top = jnp.full((heads_here, tok_rows), -jnp.inf, jnp.float32)
    start_total = jnp.zeros((heads_here, tok_rows), jnp.float32)
    (row_top, exp_total), _ = lax.scan(
        stat_step, (start_top, start_total), (key_blocks, seen_blocks, needed)
    )
    log_total = row_top + jnp.log(exp_total)

    def output_step(totals, block_item):
        key_block, value_block, seen_mask, block_needed = block_item
        scores = masked_scores(query_heads, key_block, seen_mask)
        weights = jnp.exp(scores - log_total[..., None]).astype(jnp.bfloat16)
        return (
            totals
            + jnp.einsum("hqk,khd->qhd", weights, value_block, preferred_element_type=jnp.float32),
            None,
        )

    empty_heads = jnp.zeros((tok_rows, heads_here, HD), jnp.float32)
    attended_f, _ = lax.scan(
        output_step, empty_heads, (key_blocks, value_blocks, seen_blocks, needed)
    )
    attended = attended_f.astype(jnp.bfloat16).reshape(tok_rows, feature_count)
    w_full = lax.all_gather(w_out, "seq", axis=1, tiled=True)
    partial_branch = jnp.dot(attended, w_full, preferred_element_type=jnp.float32)
    summed_branch = lax.psum_scatter(
        partial_branch.astype(jnp.bfloat16), "fsdp", scatter_dimension=1, tiled=True
    ).astype(jnp.float32)
    col_count = residual.shape[1]
    gate_here = lax.dynamic_slice_in_dim(gate, lax.axis_index("fsdp") * col_count, col_count, 0)
    layer_out = (residual.astype(jnp.float32) + gate_here[None, :] * summed_branch).astype(
        jnp.bfloat16
    )
    gated_grad = (grad_out.astype(jnp.float32) * gate[None, :]).astype(jnp.bfloat16)
    d_attended = jnp.einsum(
        "td,kd->tk", gated_grad, w_full, preferred_element_type=jnp.float32
    ).astype(jnp.bfloat16)
    weight_terms = jnp.einsum("tk,td->kd", attended, gated_grad, preferred_element_type=jnp.float32)
    d_weight = lax.psum_scatter(weight_terms, "seq", scatter_dimension=1, tiled=True)
    grad_heads = d_attended.reshape(tok_rows, heads_here, HD)
    row_delta = jnp.sum(
        grad_heads.astype(jnp.float32)
        * attended.reshape(tok_rows, heads_here, HD).astype(jnp.float32),
        axis=2,
    ).T

    def query_grad_step(totals, block_item):
        key_block, value_block, seen_mask, block_needed = block_item
        scores = masked_scores(query_heads, key_block, seen_mask)
        probability = jnp.exp(scores - log_total[..., None])
        dprobs = jnp.einsum(
            "qhd,khd->hqk", grad_heads, value_block, preferred_element_type=jnp.float32
        )
        dscores = (probability * (dprobs - row_delta[..., None])).astype(jnp.bfloat16)
        return (
            totals
            + jnp.einsum("hqk,khd->qhd", dscores, key_block, preferred_element_type=jnp.float32),
            None,
        )

    query_grad, _ = lax.scan(
        query_grad_step, empty_heads, (key_blocks, value_blocks, seen_blocks, needed)
    )
    d_queries = (query_grad * score_scale).astype(jnp.bfloat16).reshape(tok_rows, feature_count)
    key_heads = keys.reshape(tok_rows, heads_here, HD)
    value_heads = values.reshape(tok_rows, heads_here, HD)
    total_all, delta_all = (
        lax.all_gather(log_total.T, "seq", axis=0, tiled=True),
        lax.all_gather(row_delta.T, "seq", axis=0, tiled=True),
    )
    query_piece = lax.all_gather(queries, "seq", axis=0, tiled=True)
    grad_piece = lax.all_gather(d_attended, "seq", axis=0, tiled=True)
    row_count = query_piece.shape[0]
    sub_rows = math.gcd(row_count, block_rows)
    part_count = row_count // sub_rows
    block_items = (
        query_piece.reshape(part_count, sub_rows, heads_here, HD),
        grad_piece.reshape(part_count, sub_rows, heads_here, HD),
        total_all.reshape(part_count, sub_rows, heads_here),
        delta_all.reshape(part_count, sub_rows, heads_here),
        seeing_local.reshape(part_count, sub_rows // GROUP, local_count),
    )

    def key_step(running_pair, block_item):
        query_block, grad_block, total_block, delta_block, seen_mask = block_item
        key_grad, value_grad = running_pair
        scores = (
            jnp.einsum("qhd,khd->hqk", query_block, key_heads, preferred_element_type=jnp.float32)
            * score_scale
        )
        scores = jnp.where(expand(seen_mask)[None], scores, -jnp.inf)
        probability = jnp.exp(scores - total_block.T[..., None])
        dprobs = jnp.einsum(
            "qhd,khd->hqk", grad_block, value_heads, preferred_element_type=jnp.float32
        )
        dscores = (probability * (dprobs - delta_block.T[..., None])).astype(jnp.bfloat16)
        weights = probability.astype(jnp.bfloat16)
        key_grad = key_grad + jnp.einsum(
            "hqk,qhd->khd", dscores, query_block, preferred_element_type=jnp.float32
        )
        value_grad = value_grad + jnp.einsum(
            "hqk,qhd->khd", weights, grad_block, preferred_element_type=jnp.float32
        )
        return ((key_grad, value_grad), None)

    result, _ = lax.scan(key_step, (empty_heads, empty_heads), block_items)
    key_grad, value_grad = result
    d_keys = (key_grad * score_scale).astype(jnp.bfloat16).reshape(tok_rows, feature_count)
    d_values = value_grad.astype(jnp.bfloat16).reshape(tok_rows, feature_count)
    return (layer_out, d_queries, d_keys, d_values, d_weight)


def solution(mesh):
    in_specs = (
        P("seq", "fsdp"),
        P("seq", "fsdp"),
        P("seq", "fsdp"),
        P("seq", "fsdp"),
        P(),
        P("fsdp", "seq"),
        P("seq", None),
        P(),
        P(),
    )
    out_specs = (
        P("seq", "fsdp"),
        P("seq", "fsdp"),
        P("seq", "fsdp"),
        P("seq", "fsdp"),
        P("fsdp", "seq"),
    )
    return jax.shard_map(local, mesh=mesh, in_specs=in_specs, out_specs=out_specs, check_vma=False)
```

profile of v0, /device:TPU:48, one launch (start us, length us, event | category | flops | bytes accessed | tf_op | source)
XLA Modules:
  0.0 1572.2 jit_solution(13968496268610104209)
XLA Ops:
  13.3 1.4 gather_fusion
  16.4 169.7 %all_gather.23 = bf16[128,3072]{0,1:T(8,128)(2,1)S(1)} all-gather(bf16[128,48]{0,1:T(8,128)(2,1)} %param.22), channel_id=1, replica_groups=mesh['seq'=64,'fsdp'=8] {'seq'}, dimensions={1}, use_global_device_ids=true | all-gather | bytes 798720 | tf_op jit(solution)/shard_map/all_gather | solution.py:86
  186.1 131.3 %all-gather.5.cloned.1.call-done = bf16[8192,128]{1,0:T(8,128)(2,1)} async-done(((bf16[128,128]{1,0:T(8,128)(2,1)}), bf16[8192,128]{1,0:T(8,128)(2,1)}) %all-gather.5.cloned.1.call-update) | async-done | bytes 2097168 | tf_op jit(solution)/shard_map/all_gather | solution.py:37
  317.4 8.2 reshape.176
  325.6 10.6 copy.96
  336.2 283.7 %all-gather.7.cloned.1.call-done = bf16[8192,128]{1,0:T(8,128)(2,1)} async-done(((bf16[128,128]{1,0:T(8,128)(2,1)}), bf16[8192,128]{1,0:T(8,128)(2,1)}) %all-gather.7.cloned.1.call-update) | async-done | bytes 2097168 | tf_op jit(solution)/shard_map/all_gather | solution.py:36
  619.9 8.2 reshape.177
  628.1 9.1 copy.97
  637.2 15.8 %while.48 = (s32[]{:T(128)}, f32[2,128]{1,0:T(2,128)S(1)}, f32[2,128]{1,0:T(2,128)S(1)}, s32[16,2,8]{2,1,0:T(2,128)S(1)}, bf16[16,512,2,64]{1,3,2,0:T(8,128)(2,1...) while((s32[]{:T(128)}, f32[2,128]{1,0:T(2,128)S(1)}, f32[2,128]{1,0:T(2,128)S(1)}, ...), condition=%wide.region_3.4_spmd.clone, body=%wide.region_0.3_spmd.clone.sunk | while | flops 17434896 | bytes 1620176 | solution.py:66
  653.1 40.6 %while.49 = (s32[]{:T(128)}, f32[128,2,64]{0,2,1:T(8,128)}, bf16[16,512,2,64]{1,3,2,0:T(8,128)(2,1)}, s32[16,2,8]{2,1,0:T(2,128)S(1)}, bf16[16,512,2,64]{1,3,2,0...) while((s32[]{:T(128)}, f32[128,2,64]{0,2,1:T(8,128)}, ...), condition=%wide.region_5.6_spmd.clone, body=%wide.region_4.5_spmd.clone.sunk | while | flops 34111504 | bytes 821970 | solution.py:82
  653.6 2.0 fusion.122
  656.2 2.0 fusion.122
  658.7 2.0 fusion.122
  661.2 2.0 fusion.122
  663.8 2.0 fusion.122
  666.3 2.0 fusion.122
  668.9 2.0 fusion.122
  671.4 2.0 fusion.122
  673.9 2.0 fusion.122
  676.5 2.0 fusion.122
  679.0 2.0 fusion.122
  681.5 2.0 fusion.122
  684.1 2.0 fusion.122
  686.6 2.0 fusion.122
  689.1 2.0 fusion.122
  691.7 2.0 fusion.122
  693.7 2.2 multiply_reduce_fusion
  695.9 1.4 convolution_convert_fusion
  697.2 2.3 copy.115
  701.0 35.8 %while.50 = (s32[]{:T(128)}, f32[128,2,64]{0,2,1:T(8,128)S(1)}, bf16[16,512,2,64]{1,3,2,0:T(8,128)(2,1)S(1)}, s32[16,2,8]{2,1,0:T(2,128)S(1)}, bf16[128,2,64]{0,...) while((s32[]{:T(128)}, f32[128,2,64]{0,2,1:T(8,128)S(1)}, ...), condition=%wide.region_9.10_spmd.clone, body=%wide.region_8.9_spmd.clone.sunk | while | flops 51150864 | bytes 2035430 | solution.py:123
  737.5 184.7 %all-gather.9.cloned.1.call-done = bf16[8192,128]{1,0:T(8,128)(2,1)} async-done(((bf16[128,128]{1,0:T(8,128)(2,1)}), bf16[8192,128]{1,0:T(8,128)(2,1)}) %all-gather.9.cloned.1.call-update) | async-done | bytes 2097168 | tf_op jit(solution)/shard_map/all_gather | solution.py:133
  922.2 8.2 reshape.173
  930.4 10.7 copy.106
  941.1 155.8 %all_gather.27 = f32[8192,2]{0,1:T(2,128)S(1)} all-gather(f32[128,2]{0,1:T(2,128)S(1)} %bitcast.223), channel_id=1, replica_groups=mesh['seq'=64,'fsdp'=8] {'seq'}, dimensions={0}, use_global_device_ids=true | all-gather | bytes 66560 | tf_op jit(solution)/shard_map/all_gather | solution.py:131
  1096.9 150.3 %all_gather.25 = f32[8192,2]{0,1:T(2,128)S(1)} all-gather(f32[128,2]{0,1:T(2,128)S(1)} %bitcast.225), channel_id=1, replica_groups=mesh['seq'=64,'fsdp'=8] {'seq'}, dimensions={0}, use_global_device_ids=true | all-gather | bytes 66560 | tf_op jit(solution)/shard_map/all_gather | solution.py:130
  1247.2 1.6 fusion.79
  1250.6 2.4 copy.121
  1254.2 53.9 %while.51 = (s32[]{:T(128)}, f32[128,2,64]{0,2,1:T(8,128)S(1)}, f32[128,2,64]{0,2,1:T(8,128)S(1)}, bf16[16,512,2,64]{1,3,2,0:T(8,128)(2,1)}, s32[16,8,2]{1,2,0:T...) while((s32[]{:T(128)}, f32[128,2,64]{0,2,1:T(8,128)S(1)}, ...), condition=%wide.region_11.12_spmd.clone, body=%wide.region_10.11_spmd.clone.sunk | while | flops 68091920 | bytes 2844407 | solution.py:168
  1254.8 1.2 fusion.137
  1256.0 1.4 fusion.138
  1258.1 1.2 fusion.137
  1259.4 1.4 fusion.138
  1262.7 1.4 fusion.138
  1266.1 1.4 fusion.138
  1268.2 1.2 fusion.137
  1269.5 1.4 fusion.138
  1271.6 1.2 fusion.137
  1272.8 1.4 fusion.138
  1275.0 1.2 fusion.137
  1276.2 1.4 fusion.138
  1279.6 1.4 fusion.138
  1283.0 1.4 fusion.138
  1286.3 1.4 fusion.138
  1288.4 1.2 fusion.137
  1289.7 1.4 fusion.138
  1293.1 1.4 fusion.138
  1295.2 1.2 fusion.137
  1296.4 1.4 fusion.138
  1298.6 1.2 fusion.137
  1299.8 1.4 fusion.138
  1303.2 1.4 fusion.138
  1305.3 1.2 fusion.137
  1306.5 1.4 fusion.138
  1309.6 255.8 %reduce-scatter.5.cloned.1.call-done = f32[128,48]{0,1:T(8,128)} async-done(((f32[128,3072]{0,1:T(8,128)}), f32[128,48]{0,1:T(8,128)}) %reduce-scatter.5.cloned.1.call-update) | async-done | bytes 24592 | tf_op jit(solution)/shard_map/reduce_scatter | solution.py:101
  (470 shorter events, 92.3 us)
Async XLA Ops:
  7.2 310.3 %all-gather.5.cloned.1.call-start = ((), (), s32[]{:S(2)}) async-start(), calls=%async_computation.2 | async-start | bytes 2129920 | tf_op jit(solution)/shard_map/all_gather | solution.py:37
  7.9 612.0 %all-gather.7.cloned.1.call-start = ((), (), s32[]{:S(2)}) async-start(), calls=%async_computation.3 | async-start | bytes 2129920 | tf_op jit(solution)/shard_map/all_gather | solution.py:36
  8.6 913.6 %all-gather.9.cloned.1.call-start = ((), (), s32[]{:S(2)}) async-start(), calls=%async_computation.4 | async-start | bytes 2129920 | tf_op jit(solution)/shard_map/all_gather | solution.py:133
  9.4 1239.5 %reduce-scatter.7.cloned.1.call-start = ((), (), s32[]{:S(2)}) async-start(), calls=%async_computation.7 | async-start | bytes 884736
  653.1 40.6 %copy-start.5 = (f32[3072]{0:T(1024)S(1)}, f32[3072]{0:T(1024)}, u32[]{:S(2)}) copy-start(f32[3072]{0:T(1024)} %param.21) | copy-start | bytes 36868
  695.9 3.8 copy-start.2
  695.9 3.9 copy-start.3
  695.9 5.1 copy-start.1
  699.6 551.0 %all-gather.11.cloned.1.call-start = ((), (), s32[]{:S(2)}) async-start(), calls=%async_computation.5 | async-start | bytes 2129920 | tf_op jit(solution)/shard_map/all_gather | solution.py:134
  701.0 864.4 %reduce-scatter.5.cloned.1.call-start = ((), (), s32[]{:S(2)}) async-start(), calls=%async_computation.6 | async-start | bytes 1597440 | tf_op jit(solution)/shard_map/reduce_scatter | solution.py:101
  930.4 316.8 %copy-start = (bf16[128,3072]{1,0:T(8,128)(2,1)S(1)}, bf16[128,3072]{1,0:T(8,128)(2,1)}, u32[]{:S(2)}) copy-start(bf16[128,3072]{1,0:T(8,128)(2,1)} %param.23) | copy-start | bytes 2359300
  1247.2 2.7 copy-start.4
Sparse Core Ops, SparseCore 0:
  10.1 307.3 all-gather.4
  319.5 300.3 all-gather.6
  622.0 300.1 all-gather.8
  924.9 34.8 reduce-scatter.6
  962.4 246.1 all-gather.10
  1249.0 316.3 reduce-scatter.4
where the time goes:
time: 1580 us; the launch traced here: 1570 us
  waiting for transfers between devices  858 us (54%)
  blocking collectives  476 us (30%)
  matrix products  113 us (7%)
  local copies, waits for them, and re-layouts  102 us (6%)
    all_gather x1, waiting for transfers between devices, local(): lax.all_gather(keys, 'seq', axis=0, tiled=True)  284 us
    reduce_scatter x1, waiting for transfers between devices, local(): lax.psum_scatter(weight_terms, 'seq', scatter_dimension=1, tiled=True)  256 us
    all_gather x1, waiting for transfers between devices, local(): query_piece = lax.all_gather(queries, 'seq', axis=0, tiled=True)  185 us
    all_gather x1, blocking collectives, local(): w_full = lax.all_gather(w_out, 'seq', axis=1, tiled=True)  170 us
    all_gather x1, blocking collectives, local(): lax.all_gather(row_delta.T, 'seq', axis=0, tiled=True)  156 us
    all_gather x1, blocking collectives, local(): lax.all_gather(log_total.T, 'seq', axis=0, tiled=True)  150 us
    all_gather x1, waiting for transfers between devices, local(): lax.all_gather(values, 'seq', axis=0, tiled=True)  131 us
    unnamed x26, local copies, waits for them, and re-layouts  41.4 us
  transfers between devices with their start and end apart: 6, of which 4 were waited for; matrix products, arithmetic and copies ran while one was open for 14% of the time, Pallas kernels for 0%

commit v1 on v0

v1 whole, which is shorter than its diff:
```python
import jax
import jax.numpy as jnp
from jax import lax
from jax.experimental import pallas as pl
from jax.experimental.pallas import tpu as pltpu
from jax.sharding import Mesh, PartitionSpec as P

ROW = ("x", "yl")
COL = ("z",)
FSDP = ("yh", "core")
SIDE = 8
TOK = 128
BLOCK = SIDE * TOK
FEAT = 128
HEADS_HERE = 2
HD = 64
GROUP = 64
GROUPS = BLOCK // GROUP
SHARD = 48
STRIP = SIDE * SHARD
TILE = 256
MASKED = -1e30
STATS = HEADS_HERE * SIDE
VMEM = 32 * 1024 * 1024
BF = jnp.bfloat16
F32 = jnp.float32


def mm(a, b):
    return jnp.dot(a, b, preferred_element_type=F32)


def call(body, out_shape, in_specs, flops=0, data=0, exps=0, **kw):
    return pl.pallas_call(
        body,
        grid=(1,),
        in_specs=in_specs,
        out_specs=jax.tree.map(lambda s: whole(s.shape), out_shape),
        out_shape=out_shape,
        compiler_params=pltpu.CompilerParams(vmem_limit_bytes=VMEM),
        cost_estimate=pl.CostEstimate(flops=flops, bytes_accessed=data, transcendentals=exps),
        **kw,
    )


def whole(shape):
    return pl.BlockSpec(shape, lambda i: (0,) * len(shape))


def at(shape, index):
    return pl.BlockSpec(shape, lambda i: index)


def out(shape, dtype=BF):
    return jax.ShapeDtypeStruct(shape, dtype)


def swap(a, axes):
    return lax.all_to_all(a, axes, 0, 0, tiled=True)


def first_payload(k_ref, v_ref, w_ref, o_ref):
    w_t = w_ref[...].astype(F32).T.astype(BF)
    for i in range(SIDE):
        o_ref[i, 0:TOK] = k_ref[...]
        o_ref[i, TOK : 2 * TOK] = v_ref[...]
        o_ref[i, 2 * TOK : 2 * TOK + SHARD] = w_t


def second_payload(g_ref, q_ref, o_ref):
    for i in range(SIDE):
        for j in range(SIDE):
            o_ref[i, j * SHARD : (j + 1) * SHARD] = g_ref[j, 2 * TOK : 2 * TOK + SHARD]
        o_ref[i, STRIP : STRIP + TOK] = q_ref[...]


def grad_payload(gated_ref, w_ref, o_ref):
    total = jnp.zeros((TOK, FEAT), F32)
    for i in range(SIDE):
        total = total + mm(gated_ref[:, i * STRIP : (i + 1) * STRIP], w_ref[i])
    grad_t = total.T.astype(BF)
    for i in range(SIDE):
        o_ref[i] = grad_t


def key_operand(k):
    row = lax.broadcasted_iota(jnp.int32, (BLOCK, GROUPS), 0) // GROUP
    col = lax.broadcasted_iota(jnp.int32, (BLOCK, GROUPS), 1)
    return jnp.concatenate([k, (row == col).astype(F32).astype(BF)], axis=1)


def query_operand(q_t, bias, head):
    mine = lax.broadcasted_iota(jnp.int32, (FEAT, 1), 0) // HD == head
    part = jnp.where(mine, q_t.astype(F32) * HD ** (-0.5), 0.0).astype(BF)
    return jnp.concatenate([part, bias], axis=0)


def transposed(a):
    return a.astype(F32).T.astype(BF)


def forward(q_ref, k_ref, v_ref, bias_ref, o_ref, lse_ref):
    q_t = transposed(q_ref[...].reshape(BLOCK, FEAT))
    k_op = key_operand(k_ref[...].reshape(BLOCK, FEAT))
    v_t = transposed(v_ref[...].reshape(BLOCK, FEAT))
    for head in range(HEADS_HERE):
        q_op = query_operand(q_t, bias_ref[...], head)
        for tile in range(BLOCK // TILE):
            span = slice(tile * TILE, (tile + 1) * TILE)
            s = mm(k_op, q_op[:, span])
            top = jnp.max(s, axis=0, keepdims=True)
            p = jnp.exp(s - top)
            total = jnp.sum(p, axis=0, keepdims=True)
            part = mm(v_t[head * HD : (head + 1) * HD], p.astype(BF))
            o_ref[head * HD : (head + 1) * HD, span] = part / total
            lse = top + jnp.log(total)
            for c in range(TILE // TOK):
                row = head * SIDE + tile * (TILE // TOK) + c
                lse_ref[row : row + 1, :] = lse[:, c * TOK : (c + 1) * TOK]


def split3(a):
    hi = a.astype(BF)
    rest = a - hi.astype(F32)
    mid = rest.astype(BF)
    return hi, mid, (rest - mid.astype(F32)).astype(BF)


def stats_payload(o_ref, lse_ref, grad_ref, out_ref):
    rows = [None] * STATS
    for c in range(SIDE):
        part = o_ref[:, c * TOK : (c + 1) * TOK]
        product = part * grad_ref[c].astype(F32)
        for head in range(HEADS_HERE):
            rows[head * SIDE + c] = jnp.sum(
                product[head * HD : (head + 1) * HD], axis=0, keepdims=True
            )
        out_ref[c, 0:FEAT] = part.astype(BF)
    pieces = jnp.concatenate(
        split3(lse_ref[...]) + split3(jnp.concatenate(rows, axis=0)), axis=0
    )
    for c in range(SIDE):
        out_ref[c, FEAT : FEAT + 6 * STATS] = pieces


def combine(me_ref, d_ref, lse_ref, delta_ref, att_ref, weight_ref):
    def quantity(j, first):
        at_row = FEAT + first * STATS
        return sum(
            d_ref[j, at_row + i * STATS : at_row + (i + 1) * STATS].astype(F32) for i in range(3)
        )

    lse = [quantity(j, 0) for j in range(SIDE)]
    top = lse[0]
    for j in range(1, SIDE):
        top = jnp.maximum(top, lse[j])
    total = jnp.zeros_like(top)
    for j in range(SIDE):
        total = total + jnp.exp(lse[j] - top)
    all_lse = top + jnp.log(total)
    lse_ref[...] = all_lse
    delta = jnp.zeros_like(top)
    for j in range(SIDE):
        weight = jnp.exp(lse[j] - all_lse)
        weight_ref[j] = weight
        delta = delta + weight * quantity(j, 3)
    delta_ref[...] = delta
    me = me_ref[0]
    heads = []
    for head in range(HEADS_HERE):
        acc = jnp.zeros((HD, TOK), F32)
        for j in range(SIDE):
            weight = weight_ref[j, pl.ds(head * SIDE + me, 1), :]
            acc = acc + weight * d_ref[j, head * HD : (head + 1) * HD].astype(F32)
        heads.append(acc)
    att_ref[...] = jnp.concatenate(heads, axis=0).T.astype(BF)


def backward(
    q_ref, k_ref, v_ref, grad_ref, bias_ref, lse_ref, delta_ref, att_ref, gated_ref,
    e_ref, f_ref, dk_ref, dv_ref,
):
    q = q_ref[...].reshape(BLOCK, FEAT)
    k = k_ref[...].reshape(BLOCK, FEAT)
    v = v_ref[...].reshape(BLOCK, FEAT)
    q_t = transposed(q)
    k_t = transposed(k)
    k_op = key_operand(k)
    grad_t = jnp.concatenate([grad_ref[c] for c in range(SIDE)], axis=1)
    grad = transposed(grad_t)
    feat_row = lax.broadcasted_iota(jnp.int32, (FEAT, 1), 0) // HD
    feat_col = lax.broadcasted_iota(jnp.int32, (1, FEAT), 1) // HD
    dk_ref[...] = jnp.zeros_like(dk_ref)
    dv_ref[...] = jnp.zeros_like(dv_ref)
    for head in range(HEADS_HERE):
        q_op = query_operand(q_t, bias_ref[...], head)
        grad_op = jnp.where(feat_row == head, grad_t.astype(F32), 0.0).astype(BF)
        q_rows = jnp.where(feat_col == head, q.astype(F32), 0.0).astype(BF)
        grad_rows = jnp.where(feat_col == head, grad.astype(F32), 0.0).astype(BF)
        for tile in range(BLOCK // TILE):
            span = slice(tile * TILE, (tile + 1) * TILE)
            first = head * SIDE + tile * (TILE // TOK)
            lse = jnp.concatenate(
                [lse_ref[first + c : first + c + 1, :] for c in range(TILE // TOK)], axis=1
            )
            delta = jnp.concatenate(
                [delta_ref[first + c : first + c + 1, :] for c in range(TILE // TOK)], axis=1
            )
            p = jnp.exp(mm(k_op, q_op[:, span]) - lse)
            ds = (p * (mm(v, grad_op[:, span]) - delta)).astype(BF)
            dq_t = mm(k_t[head * HD : (head + 1) * HD], ds).astype(BF)
            for c in range(TILE // TOK):
                to = STRIP + head * HD
                e_ref[tile * (TILE // TOK) + c, to : to + HD] = dq_t[:, c * TOK : (c + 1) * TOK]
            dv_ref[...] += mm(p.astype(BF), grad_rows[span])
            dk_ref[...] += mm(ds, q_rows[span])
    for i in range(SIDE):
        span = slice(i * TOK, (i + 1) * TOK)
        f_ref[i, 0:TOK] = (dk_ref[span] * HD ** (-0.5)).astype(BF)
        f_ref[i, TOK : 2 * TOK] = dv_ref[span].astype(BF)
        f_ref[i, 2 * TOK : 2 * TOK + SHARD] = jnp.zeros((SHARD, FEAT), BF)
    att = att_ref[...]
    for i in range(SIDE):
        e_ref[i, 0:STRIP] = mm(gated_ref[i * STRIP : (i + 1) * STRIP], att).astype(BF)


def sum_first(e_ref, dq_ref, f_ref):
    total = e_ref[0].astype(F32)
    for i in range(1, SIDE):
        total = total + e_ref[i].astype(F32)
    dq_ref[...] = (total[STRIP:].T * HD ** (-0.5)).astype(BF)
    shards = total[:STRIP].astype(BF)
    for i in range(SIDE):
        f_ref[i] = shards[i * SHARD : (i + 1) * SHARD]


def sum_second(f_ref, dk_ref, dv_ref, dw_ref):
    total = f_ref[0].astype(F32)
    for i in range(1, SIDE):
        total = total + f_ref[i].astype(F32)
    dk_ref[...] = total[0:TOK].astype(BF)
    dv_ref[...] = total[TOK : 2 * TOK].astype(BF)
    dw_ref[...] = total[2 * TOK : 2 * TOK + SHARD].T


def local(queries, keys, values, residual, gate, w_out, grad_out, group_mask, group_of_slot):
    z = lax.axis_index(COL)
    p = lax.axis_index(ROW)

    own = whole((TOK, FEAT))
    col_spec = whole((SIDE, 2 * TOK + SHARD, FEAT))
    row_spec = whole((SIDE, STRIP + TOK, FEAT))
    sent = call(
        first_payload,
        out((SIDE, 2 * TOK + SHARD, FEAT)),
        [own, own, whole((FEAT, SHARD))],
        data=1 << 20,
    )(keys, values, w_out)
    kvw = swap(sent, COL)

    slots = group_of_slot.reshape(SIDE, SIDE, TOK // GROUP)
    query_groups = lax.dynamic_index_in_dim(slots, z, 0, keepdims=False).reshape(GROUPS)
    key_groups = lax.dynamic_index_in_dim(slots, p, 1, keepdims=False).reshape(GROUPS)
    ids = jnp.arange(group_mask.shape[0], dtype=jnp.int32)
    query_hot = (query_groups[:, None] == ids[None, :]).astype(BF)
    key_hot = (key_groups[:, None] == ids[None, :]).astype(BF)
    picked = jnp.einsum(
        "qa,ab->bq", query_hot, (group_mask == 1).astype(BF), preferred_element_type=F32
    ).astype(BF)
    table = jnp.einsum("kb,bq->kq", key_hot, picked, preferred_element_type=F32)
    bias = jnp.where(table > 0.5, 0.0, MASKED).astype(BF)
    bias = jnp.broadcast_to(bias[:, :, None], (GROUPS, GROUPS, GROUP)).reshape(GROUPS, BLOCK)

    gated = (grad_out.astype(F32) * gate[None, :]).astype(BF)
    gated = gated.reshape(TOK, SIDE, SIDE, SHARD).transpose(0, 2, 1, 3).reshape(TOK, SIDE * STRIP)
    gated_t = gated.T

    sent = call(
        second_payload,
        out((SIDE, STRIP + TOK, FEAT)),
        [col_spec, own],
        data=2 << 20,
    )(kvw, queries)
    wq = swap(sent, ROW)

    sent = call(
        grad_payload,
        out((SIDE, FEAT, TOK)),
        [whole((TOK, SIDE * STRIP)), at((SIDE, STRIP, FEAT), (0, 0, 0))],
        flops=2 * TOK * FEAT * SIDE * STRIP,
        data=2 << 20,
    )(gated, wq)
    grad_t = swap(sent, ROW)

    query_spec = at((SIDE, TOK, FEAT), (0, STRIP // TOK, 0))
    key_spec = at((SIDE, TOK, FEAT), (0, 0, 0))
    value_spec = at((SIDE, TOK, FEAT), (0, 1, 0))
    bias_spec = whole((GROUPS, BLOCK))
    stat_spec = whole((STATS, TOK))
    pair_count = HEADS_HERE * BLOCK * BLOCK
    part, part_lse = call(
        forward,
        (out((FEAT, BLOCK), F32), out((STATS, TOK), F32)),
        [query_spec, key_spec, value_spec, bias_spec],
        flops=16 * HD * pair_count,
        data=2 << 20,
        exps=pair_count,
    )(wq, kvw, kvw, bias)
    sent = call(
        stats_payload,
        out((SIDE, FEAT + 6 * STATS, TOK)),
        [whole((FEAT, BLOCK)), stat_spec, whole((SIDE, FEAT, TOK))],
        data=2 << 20,
    )(part, part_lse, grad_t)
    parts = swap(sent, ROW)

    w_rows = (
        wq[:, :STRIP]
        .reshape(SIDE, SIDE, SHARD, FEAT)
        .transpose(1, 0, 2, 3)
        .reshape(SIDE * STRIP, FEAT)
    )
    lse, delta, attended = call(
        combine,
        (out((STATS, TOK), F32), out((STATS, TOK), F32), out((TOK, FEAT))),
        [pl.BlockSpec(memory_space=pltpu.SMEM), whole((SIDE, FEAT + 6 * STATS, TOK))],
        data=1 << 20,
        scratch_shapes=[pltpu.VMEM((SIDE, STATS, TOK), F32)],
    )(p.reshape(1).astype(jnp.int32), parts)
    branch = jnp.einsum("dk,tk->dt", w_rows, attended, preferred_element_type=F32).astype(BF)
    summed = lax.psum_scatter(branch, FSDP, scatter_dimension=0, tiled=True)

    sent_row, sent_col = call(
        backward,
        (out((SIDE, STRIP + TOK, FEAT)), out((SIDE, 2 * TOK + SHARD, FEAT))),
        [
            query_spec,
            key_spec,
            value_spec,
            whole((SIDE, FEAT, TOK)),
            bias_spec,
            stat_spec,
            stat_spec,
            whole((TOK, FEAT)),
            whole((SIDE * STRIP, TOK)),
        ],
        flops=40 * HD * pair_count,
        data=5 << 20,
        exps=pair_count,
        scratch_shapes=[pltpu.VMEM((BLOCK, FEAT), F32)] * 2,
    )(wq, kvw, kvw, grad_t, bias, lse, delta, attended, gated_t)
    got_row = swap(sent_row, ROW)
    d_queries, shards = call(
        sum_first,
        (out((TOK, FEAT)), out((SIDE, SHARD, FEAT))),
        [row_spec],
        data=2 << 20,
    )(got_row)
    sent_col = jnp.concatenate([sent_col[:, : 2 * TOK], shards], axis=1)
    got_col = swap(sent_col, COL)
    d_keys, d_values, d_weight = call(
        sum_second,
        (out((TOK, FEAT)), out((TOK, FEAT)), out((FEAT, SHARD), F32)),
        [col_spec],
        data=1 << 20,
    )(got_col)

    col_count = residual.shape[1]
    gate_here = lax.dynamic_slice_in_dim(gate, lax.axis_index(FSDP) * col_count, col_count, 0)
    layer_out = (
        residual.astype(F32) + gate_here[None, :] * summed.astype(F32).T
    ).astype(BF)
    return (layer_out, d_queries, d_keys, d_values, d_weight)


def solution(mesh):
    fine = Mesh(mesh.devices.reshape(8, 4, 2, 4, 2), ("z", "x", "yl", "yh", "core"))
    seq = COL + ROW
    tile = P(seq, FSDP)
    in_specs = (tile, tile, tile, tile, P(), P(FSDP, seq), P(seq, None), P(), P())
    out_specs = (tile, tile, tile, tile, P(FSDP, seq))
    return jax.shard_map(local, mesh=fine, in_specs=in_specs, out_specs=out_specs, check_vma=False)
```

time: 1580 us -> 149 us (0.09)
  the two profiles are of different devices: /device:TPU:48 before, /device:TPU:17 now
where the time goes in v1:
time: 149 us; the launch traced here: 148 us
  waiting for transfers between devices  48.8 us (33%)
  blocking collectives  40.4 us (27%)
  starting transfers between devices  17.7 us (12%)
  Pallas kernels  16.2 us (11%)
  between operations  14.2 us (10%)
  local copies, waits for them, and re-layouts  6.51 us (4%)
  other arithmetic  2.35 us (2%)
  matrix products  1.62 us (1%)
    all_to_all x2, blocking collectives, swap(): return lax.all_to_all(a, axes, 0, 0, tiled=True)  40.4 us
    reduce_scatter x1, waiting for transfers between devices, local(): summed = lax.psum_scatter(branch, FSDP, scatter_dimension=0, tiled=True)  27.7 us
    all_to_all x4, waiting for transfers between devices, swap(): return lax.all_to_all(a, axes, 0, 0, tiled=True)  21.1 us
    all_to_all x4, starting transfers between devices, swap(): return lax.all_to_all(a, axes, 0, 0, tiled=True)  17.6 us
    pallas_call x1, Pallas kernels, local(): call(backward, (out((SIDE, STRIP + TOK, FEAT)), out((SIDE, 2 * TOK + SHAR...  6.24 us
    pallas_call x1, Pallas kernels, local(): call(forward, (out((FEAT, BLOCK), F32), out((STATS, TOK), F32)), [query_s...  5.79 us
    unnamed x23, local copies, waits for them, and re-layouts  5.43 us
  transfers between devices with their start and end apart: 5, of which 3 were waited for; matrix products, arithmetic and copies ran while one was open for 4% of the time, Pallas kernels for 4%

profile of v1, /device:TPU:17, one launch (start us, length us, event | category | flops | bytes accessed | tf_op | source)
XLA Modules:
  0.0 147.8 jit_solution(15868059813195793903)
XLA Ops:
  7.2 0.0 copy-start.3
  7.2 0.8 copy.21.w_ref
  8.0 0.0 copy-start.1
  8.0 0.8 copy-done.1
  8.8 0.0 copy-start.2
  8.8 0.8 copy-done.2
  9.5 0.1 shard_map.128
  9.6 28.4 %all_to_all.30.g_ref.k_ref.v_ref = bf16[8,304,128]{2,1,0:T(8,128)(2,1)S(1)} all-to-all(bf16[8,304,128]{2,1,0:T(8,128)(2,1)S(1)} %shard_map.128), channel_id=1, replica_groups=mesh['z'=8,'x'=4,'yl'=2,'yh'=4,'core'=2] {'z'}, dimensions={0} | all-to-all | bytes 1245184 | tf_op jit(solution)/shard_map/all_to_all | solution.py:59
  38.0 0.0 copy-done.3
  38.0 1.1 shard_map.129
  39.1 0.0 copy-start.7
  39.1 0.0 copy-start.4
  39.1 5.2 %all-to-all-start.1 = ((bf16[8,512,128]{2,1,0:T(8,128)(2,1)}), bf16[8,512,128]{2,1,0:T(8,128)(2,1)S(1)}, u32[]{:S(2)}, u32[]{:S(2)}) async-start(bf16[8,512,128]{2,1,0:T(8,128)(2,1)} %shard_map.129), calls=%async_computation.1 | async-start | bytes 2097152 | tf_op jit(solution)/shard_map/all_to_all | solution.py:59
  44.3 0.0 copy-start.6
  44.3 0.0 copy-done.7
  44.3 0.1 reshape.41
  44.5 0.0 copy-done.4
  44.5 0.4 copy.23
  44.8 0.2 copy-done.6
  45.0 0.5 multiply_convert_fusion
  45.5 0.1 copy.24
  45.5 0.3 copy.25.gated_ref
  45.8 0.0 copy-start.8
  45.8 12.0 %all-to-all-done.1.q_ref.w_ref = bf16[8,512,128]{2,1,0:T(8,128)(2,1)S(1)} async-done(((bf16[8,512,128]{2,1,0:T(8,128)(2,1)}), bf16[8,512,128]{2,1,0:T(8,128)(2,1)S(1)}, u32[]{:S(2)}, u32[]{:S(2)}) %all-to-all-start.1) | async-done | bytes 1048608 | tf_op jit(solution)/shard_map/all_to_all | solution.py:59
  57.8 1.2 shard_map.131
  59.0 3.4 %all-to-all-start.2 = ((bf16[8,128,128]{2,1,0:T(8,128)(2,1)}), bf16[8,128,128]{2,1,0:T(8,128)(2,1)S(1)}, u32[]{:S(2)}, u32[]{:S(2)}) async-start(bf16[8,128,128]{2,1,0:T(8,128)(2,1)} %shard_map.131), calls=%async_computation.2 | async-start | bytes 524288 | tf_op jit(solution)/shard_map/all_to_all | solution.py:59
  62.5 0.1 eq.36
  62.6 0.1 eq.42
  62.6 0.0 copy-done.8
  62.6 0.3 fusion.3
  63.0 0.1 broadcast_in_dim.20
  63.1 0.1 reshape.42.bias_ref
  63.2 5.8 %shard_map.130 = (f32[128,1024]{1,0:T(8,128)S(1)}, f32[16,128]{1,0:T(8,128)S(1)}) custom-call(bf16[8,512,128]{2,1,0:T(8,128)(2,1)S(1)} %all-to-all-done.1.q_ref.w_ref, bf16[8,304,128]{2,1,0:T(8,128)(2,1)S(1)} %all_to_all.30.g_ref.k_ref.v_ref, bf16[8,304,128]{2,1,0:T(8,128)(2,1)S(1)} %all_to_all.30.g_ref.k_ref.v_ref, bf16[16,1024]{1,0:T(8,128)(2,1)S(1)} %reshape.42.bias_ref), custom_call_target="tpu_custom_call" | custom-call | flops 2147483648 | bytes 2097152 | tf_op jit(solution)/shard_map/pallas_call | solution.py:301
  69.0 0.0 all-to-all-done.2.grad_ref
  69.0 0.1 shard_map.132
  69.1 12.1 %all_to_all.31.d_ref = bf16[8,224,128]{2,1,0:T(8,128)(2,1)S(1)} all-to-all(bf16[8,224,128]{2,1,0:T(8,128)(2,1)S(1)} %shard_map.132), channel_id=1, replica_groups=mesh['z'=8,'x'=4,'yl'=2,'yh'=4,'core'=2] {'x','yl'}, dimensions={0} | all-to-all | bytes 917504 | tf_op jit(solution)/shard_map/all_to_all | solution.py:59
  81.2 0.2 shard_map.133
  81.3 6.2 %shard_map.134 = (bf16[8,512,128]{2,1,0:T(8,128)(2,1)S(1)}, bf16[8,304,128]{2,1,0:T(8,128)(2,1)S(1)}) custom-call(bf16[8,512,128]{2,1,0:T(8,128)(2,1)S(1)} %all-to-all-done.1.q_ref.w_ref, bf16[8,304,128]{2,1,0:T(8,128)(2,1)S(1)} %all_to_all.30.g_ref.k_ref.v_ref, bf16[8,304,128]{2,1,0:T(8,128)(2,1)S(1)} %all_to_all.30.g_ref.k_ref.v_ref, ...), custom_call_target="tpu_custom_call" | custom-call | flops 5368709120 | bytes 5242880 | tf_op jit(solution)/shard_map/pallas_call | solution.py:333
  87.6 0.0 copy-start
  87.6 1.0 copy-done
  88.6 3.6 %all-to-all-start.4 = ((bf16[8,512,128]{2,1,0:T(8,128)(2,1)}), bf16[8,512,128]{2,1,0:T(8,128)(2,1)S(1)}, u32[]{:S(2)}, u32[]{:S(2)}) async-start(bf16[8,512,128]{2,1,0:T(8,128)(2,1)} %copy-done), calls=%async_computation.5 | async-start | bytes 2097152 | tf_op jit(solution)/shard_map/all_to_all | solution.py:59
  92.1 0.0 reduce-scatter.2.cloned.1.call-start
  92.2 0.1 slice.8
  92.2 0.1 copy.22
  92.3 1.3 convolution_convert_fusion
  93.6 0.0 reduce-scatter.2.cloned.1.call-update
  93.7 9.1 %all-to-all-done.4.e_ref = bf16[8,512,128]{2,1,0:T(8,128)(2,1)S(1)} async-done(((bf16[8,512,128]{2,1,0:T(8,128)(2,1)}), bf16[8,512,128]{2,1,0:T(8,128)(2,1)S(1)}, u32[]{:S(2)}, u32[]{:S(2)}) %all-to-all-start.4) | async-done | bytes 1048608 | tf_op jit(solution)/shard_map/all_to_all | solution.py:59
  102.7 0.8 shard_map.135
  103.6 0.0 copy-start.5
  103.6 0.9 pad_maximum_fusion
  104.4 5.5 %all-to-all-start.5 = ((bf16[8,304,128]{2,1,0:T(8,128)(2,1)}), bf16[8,304,128]{2,1,0:T(8,128)(2,1)S(1)}, u32[]{:S(2)}, u32[]{:S(2)}) async-start(bf16[8,304,128]{2,1,0:T(8,128)(2,1)} %pad_maximum_fusion), calls=%async_computation.6 | async-start | bytes 1245184 | tf_op jit(solution)/shard_map/all_to_all | solution.py:59
  109.9 0.1 dynamic_slice.11
  110.0 0.0 copy-done.5
  110.0 0.1 copy.20
  110.1 27.7 %reduce-scatter.2.cloned.1.call-done = bf16[384,128]{1,0:T(8,128)(2,1)} async-done(((bf16[3072,128]{1,0:T(8,128)(2,1)}), bf16[384,128]{1,0:T(8,128)(2,1)}) %reduce-scatter.2.cloned.1.call-update) | async-done | bytes 98320 | tf_op jit(solution)/shard_map/reduce_scatter | solution.py:331
  137.8 1.0 fusion.4
  138.8 0.8 copy.26
  139.6 0.0 all-to-all-done.5.f_ref
  139.6 0.7 shard_map.136
  140.3 0.7 copy.27
  (3 shorter events, 0.1 us)
Async XLA Ops:
  7.2 30.8 %copy-start.3 = (bf16[128,128]{1,0:T(8,128)(2,1)S(1)}, bf16[128,128]{1,0:T(8,128)(2,1)}, u32[]{:S(2)}) copy-start(bf16[128,128]{1,0:T(8,128)(2,1)} %q_ref.1) | copy-start | bytes 98308
  8.0 0.8 copy-start.1
  8.8 0.8 copy-start.2
  39.1 5.2 %copy-start.7 = (s32[128]{0:T(128)S(1)}, s32[128]{0:T(128)}, u32[]{:S(2)}) copy-start(s32[128]{0:T(128)} %param.17) | copy-start | bytes 1540
  39.1 5.3 %copy-start.4 = (bf16[128,3072]{1,0:T(8,128)(2,1)S(1)}, bf16[128,3072]{1,0:T(8,128)(2,1)}, u32[]{:S(2)}) copy-start(bf16[128,3072]{1,0:T(8,128)(2,1)} %param.15) | copy-start | bytes 2359300
  39.1 18.7 %all-to-all-start.1 = ((bf16[8,512,128]{2,1,0:T(8,128)(2,1)}), bf16[8,512,128]{2,1,0:T(8,128)(2,1)S(1)}, u32[]{:S(2)}, u32[]{:S(2)}) async-start(bf16[8,512,128]{2,1,0:T(8,128)(2,1)} %shard_map.129), calls=%async_computation.1 | async-start | bytes 2097152 | tf_op jit(solution)/shard_map/all_to_all | solution.py:59
  44.3 0.7 copy-start.6
  45.8 16.8 %copy-start.8 = (s32[128,128]{1,0:T(8,128)S(1)}, s32[128,128]{1,0:T(8,128)}, u32[]{:S(2)}) copy-start(s32[128,128]{1,0:T(8,128)} %param.16) | copy-start | bytes 196612
  59.0 10.0 %all-to-all-start.2 = ((bf16[8,128,128]{2,1,0:T(8,128)(2,1)}), bf16[8,128,128]{2,1,0:T(8,128)(2,1)S(1)}, u32[]{:S(2)}, u32[]{:S(2)}) async-start(bf16[8,128,128]{2,1,0:T(8,128)(2,1)} %shard_map.131), calls=%async_computation.2 | async-start | bytes 524288 | tf_op jit(solution)/shard_map/all_to_all | solution.py:59
  87.6 1.0 copy-start
  88.6 14.2 %all-to-all-start.4 = ((bf16[8,512,128]{2,1,0:T(8,128)(2,1)}), bf16[8,512,128]{2,1,0:T(8,128)(2,1)S(1)}, u32[]{:S(2)}, u32[]{:S(2)}) async-start(bf16[8,512,128]{2,1,0:T(8,128)(2,1)} %copy-done), calls=%async_computation.5 | async-start | bytes 2097152 | tf_op jit(solution)/shard_map/all_to_all | solution.py:59
  92.1 45.7 %reduce-scatter.2.cloned.1.call-start = ((), (), s32[]{:S(2)}) async-start(), calls=%async_computation.7 | async-start | bytes 884736 | tf_op jit(solution)/shard_map/reduce_scatter | solution.py:331
  103.6 6.4 %copy-start.5 = (bf16[128,384]{1,0:T(8,128)(2,1)S(1)}, bf16[128,384]{1,0:T(8,128)(2,1)}, u32[]{:S(2)}) copy-start(bf16[128,384]{1,0:T(8,128)(2,1)} %param.12) | copy-start | bytes 294916
  104.4 35.1 %all-to-all-start.5 = ((bf16[8,304,128]{2,1,0:T(8,128)(2,1)}), bf16[8,304,128]{2,1,0:T(8,128)(2,1)S(1)}, u32[]{:S(2)}, u32[]{:S(2)}) async-start(bf16[8,304,128]{2,1,0:T(8,128)(2,1)} %pad_maximum_fusion), calls=%async_computation.6 | async-start | bytes 1245184 | tf_op jit(solution)/shard_map/all_to_all | solution.py:59
Sparse Core Ops, SparseCore 0:
  95.8 41.9 reduce-scatter.1

commit v2 on v1

v2 whole, which is shorter than its diff:
```python
import jax
import jax.numpy as jnp
from jax import lax
from jax.experimental import pallas as pl
from jax.experimental.pallas import tpu as pltpu
from jax.sharding import Mesh, PartitionSpec as P

ROW = ("x", "yl")
COL = ("z",)
FSDP = ("yh", "core")
SIDE = 8
PAIRS = 4
TOK = 128
BLOCK = SIDE * TOK
FEAT = 128
HEADS_HERE = 2
HD = 64
GROUP = 64
GROUPS = BLOCK // GROUP
SHARD = 48
STRIP = SIDE * SHARD
TILE = 256
MASKED = -1e30
STATS = HEADS_HERE * SIDE
VMEM = 32 * 1024 * 1024
BF = jnp.bfloat16
F32 = jnp.float32


def mm(a, b):
    return jnp.dot(a, b, preferred_element_type=F32)


def call(body, out_shape, in_specs, flops=1, data=1, exps=0, out_specs=None, grid=(1,), **kw):
    if out_specs is None:
        out_specs = jax.tree.map(lambda s: whole(s.shape), out_shape)
    return pl.pallas_call(
        body,
        grid=grid,
        in_specs=in_specs,
        out_specs=out_specs,
        out_shape=out_shape,
        compiler_params=pltpu.CompilerParams(vmem_limit_bytes=VMEM),
        cost_estimate=pl.CostEstimate(flops=flops, bytes_accessed=data, transcendentals=exps),
        **kw,
    )


def hbm(*arrays):
    return [pltpu.with_memory_space_constraint(a, pltpu.HBM) for a in arrays]


def whole(shape):
    return pl.BlockSpec(shape, lambda i: (0,) * len(shape))


def at(shape, index):
    return pl.BlockSpec(shape, lambda i: index)


def out(shape, dtype=BF):
    return jax.ShapeDtypeStruct(shape, dtype)


def far(shape, dtype=BF):
    return pltpu.HBM(shape, dtype)


def swap(a, axes):
    return lax.all_to_all(a, axes, 0, 0, tiled=True)


def repeat(block_ref, o_ref, sems):
    copies = [pltpu.make_async_copy(block_ref, o_ref.at[i], sems.at[i]) for i in range(SIDE)]
    for copy in copies:
        copy.start()
    for copy in copies:
        copy.wait()


def first_payload(k_ref, v_ref, w_ref, o_ref, block_ref, sems):
    block_ref[0:TOK] = k_ref[...]
    block_ref[TOK : 2 * TOK] = v_ref[...]
    block_ref[2 * TOK : 2 * TOK + SHARD] = w_ref[...]
    repeat(block_ref, o_ref, sems)


def second_payload(g_ref, q_ref, o_ref, block_ref, sems):
    for j in range(SIDE):
        block_ref[j * SHARD : (j + 1) * SHARD] = g_ref[j, 2 * TOK : 2 * TOK + SHARD]
    block_ref[STRIP : STRIP + TOK] = q_ref[...]
    repeat(block_ref, o_ref, sems)


def grad_payload(gated_ref, w_ref, o_ref, block_ref, sems):
    total = jnp.zeros((TOK, FEAT), F32)
    for i in range(SIDE):
        total = total + mm(gated_ref[:, i * STRIP : (i + 1) * STRIP], w_ref[i])
    block_ref[...] = total.T.astype(BF)
    repeat(block_ref, o_ref, sems)


def key_operand(k):
    row = lax.broadcasted_iota(jnp.int32, (BLOCK, GROUPS), 0) // GROUP
    col = lax.broadcasted_iota(jnp.int32, (BLOCK, GROUPS), 1)
    return jnp.concatenate([k, (row == col).astype(F32).astype(BF)], axis=1)


def query_operand(q_t, bias, head):
    mine = lax.broadcasted_iota(jnp.int32, (FEAT, 1), 0) // HD == head
    part = jnp.where(mine, q_t.astype(F32) * HD ** (-0.5), 0.0).astype(BF)
    return jnp.concatenate([part, bias], axis=0)


def transposed(a):
    return a.astype(F32).T.astype(BF)


def row_of(ref, head, tile):
    first = head * SIDE + tile * (TILE // TOK)
    return jnp.concatenate([ref[first + c : first + c + 1, :] for c in range(TILE // TOK)], axis=1)


def forward(q_ref, k_ref, v_ref, bias_ref, o_ref, mean_ref, lse_ref):
    q_t = transposed(q_ref[...].reshape(BLOCK, FEAT))
    k = k_ref[...].reshape(BLOCK, FEAT)
    k_op = key_operand(k)
    k_t = transposed(k)
    v_t = transposed(v_ref[...].reshape(BLOCK, FEAT))
    for head in range(HEADS_HERE):
        rows = slice(head * HD, (head + 1) * HD)
        q_op = query_operand(q_t, bias_ref[...], head)
        both = jnp.concatenate([v_t[rows], k_t[rows]], axis=0)
        for tile in range(BLOCK // TILE):
            span = slice(tile * TILE, (tile + 1) * TILE)
            s = mm(k_op, q_op[:, span])
            top = jnp.max(s, axis=0, keepdims=True)
            p = jnp.exp(s - top)
            total = jnp.sum(p, axis=0, keepdims=True)
            part = mm(both, p.astype(BF)) * (1.0 / total)
            o_ref[rows, span] = part[:HD].astype(BF)
            mean_ref[rows, span] = part[HD:].astype(BF)
            lse = top + jnp.log(total)
            for c in range(TILE // TOK):
                row = head * SIDE + tile * (TILE // TOK) + c
                lse_ref[row : row + 1, :] = lse[:, c * TOK : (c + 1) * TOK]


def split3(a):
    hi = a.astype(BF)
    rest = a - hi.astype(F32)
    mid = rest.astype(BF)
    return hi, mid, (rest - mid.astype(F32)).astype(BF)


def stats_payload(o_ref, lse_ref, grad_ref, out_ref, delta_ref):
    for c in range(SIDE):
        part = o_ref[:, c * TOK : (c + 1) * TOK]
        product = part.astype(F32) * grad_ref[c].astype(F32)
        for head in range(HEADS_HERE):
            row = head * SIDE + c
            delta_ref[row : row + 1, :] = jnp.sum(
                product[head * HD : (head + 1) * HD], axis=0, keepdims=True
            )
        out_ref[c, 0:FEAT] = part
    pieces = jnp.concatenate(split3(lse_ref[...]) + split3(delta_ref[...]), axis=0)
    for c in range(SIDE):
        out_ref[c, FEAT : FEAT + 6 * STATS] = pieces


def query_grad(q_ref, k_ref, v_ref, grad_ref, bias_ref, lse_ref, delta_ref, o_ref):
    k = k_ref[...].reshape(BLOCK, FEAT)
    v = v_ref[...].reshape(BLOCK, FEAT)
    q_t = transposed(q_ref[...].reshape(BLOCK, FEAT))
    k_t = transposed(k)
    k_op = key_operand(k)
    grad_t = jnp.concatenate([grad_ref[c] for c in range(SIDE)], axis=1)
    feat_row = lax.broadcasted_iota(jnp.int32, (FEAT, 1), 0) // HD
    for head in range(HEADS_HERE):
        rows = slice(head * HD, (head + 1) * HD)
        q_op = query_operand(q_t, bias_ref[...], head)
        grad_op = jnp.where(feat_row == head, grad_t.astype(F32), 0.0).astype(BF)
        for tile in range(BLOCK // TILE):
            span = slice(tile * TILE, (tile + 1) * TILE)
            p = jnp.exp(mm(k_op, q_op[:, span]) - row_of(lse_ref, head, tile))
            ds = (p * (mm(v, grad_op[:, span]) - row_of(delta_ref, head, tile))).astype(BF)
            o_ref[rows, span] = mm(k_t[rows], ds).astype(BF)


def combine(me_ref, d_ref, lse_ref, delta_ref, att_ref, weight_ref):
    def quantity(j, first):
        at_row = FEAT + first * STATS
        return sum(
            d_ref[j, at_row + i * STATS : at_row + (i + 1) * STATS].astype(F32) for i in range(3)
        )

    lse = [quantity(j, 0) for j in range(SIDE)]
    top = lse[0]
    for j in range(1, SIDE):
        top = jnp.maximum(top, lse[j])
    total = jnp.zeros_like(top)
    for j in range(SIDE):
        total = total + jnp.exp(lse[j] - top)
    all_lse = top + jnp.log(total)
    lse_ref[...] = all_lse
    delta = jnp.zeros_like(top)
    for j in range(SIDE):
        weight = jnp.exp(lse[j] - all_lse)
        weight_ref[j] = weight
        delta = delta + weight * quantity(j, 3)
    delta_ref[...] = delta
    me = me_ref[0]
    heads = []
    for head in range(HEADS_HERE):
        acc = jnp.zeros((HD, TOK), F32)
        for j in range(SIDE):
            weight = weight_ref[j, pl.ds(head * SIDE + me, 1), :]
            acc = acc + weight * d_ref[j, head * HD : (head + 1) * HD].astype(F32)
        heads.append(acc)
    att_ref[...] = jnp.concatenate(heads, axis=0).T.astype(BF)


def branch_rows(core_ref, att_ref, w_ref, keep_ref, send_ref, all_ref):
    att = att_ref[...]
    for i in range(SIDE):
        part = lax.dot_general(
            w_ref[i], att, (((1,), (1,)), ((), ())), preferred_element_type=F32
        ).astype(BF)
        for j in range(SIDE):
            all_ref[j, i * SHARD : (i + 1) * SHARD] = part[j * SHARD : (j + 1) * SHARD]
    core = core_ref[0]
    for i in range(PAIRS):
        keep_ref[i] = all_ref[2 * i + core]
        send_ref[i] = all_ref[2 * i + 1 - core]


def add_halves(pair_ref, keep_ref, got_ref, *out_refs):
    for d, o_ref in enumerate(out_refs):
        i = lax.rem(pair_ref[0] + d, PAIRS)
        o_ref[...] = (keep_ref[i].astype(F32) + got_ref[i].astype(F32)).astype(BF)


def row_payload(
    grad_ref, mean_ref, lse_ref, delta_ref, all_lse_ref, all_delta_ref, att_ref, gated_ref, e_ref
):
    att = att_ref[...]
    for i in range(SIDE):
        cols = slice(i * TOK, (i + 1) * TOK)
        for head in range(HEADS_HERE):
            rows = slice(head * HD, (head + 1) * HD)
            row = slice(head * SIDE + i, head * SIDE + i + 1)
            weight = jnp.exp(lse_ref[row, :] - all_lse_ref[row, :])
            shift = all_delta_ref[row, :] - delta_ref[row, :]
            part = grad_ref[rows, cols].astype(F32) - shift * mean_ref[rows, cols].astype(F32)
            e_ref[i, STRIP + head * HD : STRIP + (head + 1) * HD] = (weight * part).astype(BF)
        e_ref[i, 0:STRIP] = mm(gated_ref[i * STRIP : (i + 1) * STRIP], att).astype(BF)


def key_grads(
    q_ref, k_ref, v_ref, grad_ref, bias_ref, lse_ref, delta_ref, f_ref, dk_ref, dv_ref
):
    q = q_ref[...].reshape(BLOCK, FEAT)
    k = k_ref[...].reshape(BLOCK, FEAT)
    v = v_ref[...].reshape(BLOCK, FEAT)
    q_t = transposed(q)
    k_op = key_operand(k)
    grad_t = jnp.concatenate([grad_ref[c] for c in range(SIDE)], axis=1)
    grad = transposed(grad_t)
    feat_row = lax.broadcasted_iota(jnp.int32, (FEAT, 1), 0) // HD
    feat_col = lax.broadcasted_iota(jnp.int32, (1, FEAT), 1) // HD
    dk_ref[...] = jnp.zeros_like(dk_ref)
    dv_ref[...] = jnp.zeros_like(dv_ref)
    for head in range(HEADS_HERE):
        q_op = query_operand(q_t, bias_ref[...], head)
        grad_op = jnp.where(feat_row == head, grad_t.astype(F32), 0.0).astype(BF)
        q_rows = jnp.where(feat_col == head, q.astype(F32), 0.0).astype(BF)
        grad_rows = jnp.where(feat_col == head, grad.astype(F32), 0.0).astype(BF)
        for tile in range(BLOCK // TILE):
            span = slice(tile * TILE, (tile + 1) * TILE)
            p = jnp.exp(mm(k_op, q_op[:, span]) - row_of(lse_ref, head, tile))
            ds = (p * (mm(v, grad_op[:, span]) - row_of(delta_ref, head, tile))).astype(BF)
            dv_ref[...] += mm(p.astype(BF), grad_rows[span])
            dk_ref[...] += mm(ds, q_rows[span])
    for i in range(SIDE):
        span = slice(i * TOK, (i + 1) * TOK)
        f_ref[i, 0:TOK] = (dk_ref[span] * HD ** (-0.5)).astype(BF)
        f_ref[i, TOK : 2 * TOK] = dv_ref[span].astype(BF)
        f_ref[i, 2 * TOK : 2 * TOK + SHARD] = jnp.zeros((SHARD, FEAT), BF)


def sum_first(e_ref, f_in, dq_ref, f_ref, shard_ref, sem):
    del f_in
    total = e_ref[0].astype(F32)
    for i in range(1, SIDE):
        total = total + e_ref[i].astype(F32)
    shards = total[:STRIP].astype(BF)
    for i in range(SIDE):
        shard_ref[i] = shards[i * SHARD : (i + 1) * SHARD]
    copy = pltpu.make_async_copy(shard_ref, f_ref.at[:, 2 * TOK : 2 * TOK + SHARD], sem)
    copy.start()
    dq_ref[...] = (total[STRIP:].T * HD ** (-0.5)).astype(BF)
    copy.wait()


def sum_second(f_ref, dk_ref, dv_ref, dw_ref):
    total = f_ref[0].astype(F32)
    for i in range(1, SIDE):
        total = total + f_ref[i].astype(F32)
    dk_ref[...] = total[0:TOK].astype(BF)
    dv_ref[...] = total[TOK : 2 * TOK].astype(BF)
    dw_ref[...] = total[2 * TOK : 2 * TOK + SHARD]


def finish(residual_ref, gate_ref, *refs):
    total = refs[0][...].astype(F32)
    for ref in refs[1:-1]:
        total = total + ref[...].astype(F32)
    refs[-1][...] = (residual_ref[...].astype(F32) + gate_ref[...] * total.T).astype(BF)


def local(queries, keys, values, residual, gate, w_out, grad_out, group_mask, group_of_slot):
    z = lax.axis_index(COL)
    p = lax.axis_index(ROW)
    anywhere = pl.BlockSpec(memory_space=pl.ANY)

    def scratch(rows):
        return [pltpu.VMEM((rows, FEAT), BF), pltpu.SemaphoreType.DMA((SIDE,))]

    own = whole((TOK, FEAT))
    col_spec = whole((SIDE, 2 * TOK + SHARD, FEAT))
    row_spec = whole((SIDE, STRIP + TOK, FEAT))
    sent = call(
        first_payload,
        far((SIDE, 2 * TOK + SHARD, FEAT)),
        [own, own, whole((SHARD, FEAT))],
        data=1 << 20,
        out_specs=anywhere,
        scratch_shapes=scratch(2 * TOK + SHARD),
    )(*hbm(keys, values, w_out.T))
    kvw = swap(sent, COL)

    slots = group_of_slot.reshape(SIDE, SIDE, TOK // GROUP)
    query_groups = lax.dynamic_index_in_dim(slots, z, 0, keepdims=False).reshape(GROUPS)
    key_groups = lax.dynamic_index_in_dim(slots, p, 1, keepdims=False).reshape(GROUPS)
    ids = jnp.arange(group_mask.shape[0], dtype=jnp.int32)
    query_hot = (query_groups[:, None] == ids[None, :]).astype(BF)
    key_hot = (key_groups[:, None] == ids[None, :]).astype(BF)
    picked = jnp.einsum(
        "qa,ab->bq", query_hot, (group_mask == 1).astype(BF), preferred_element_type=F32
    ).astype(BF)
    table = jnp.einsum("kb,bq->kq", key_hot, picked, preferred_element_type=F32)
    bias = jnp.where(table > 0.5, 0.0, MASKED).astype(BF)
    bias = jnp.broadcast_to(bias[:, :, None], (GROUPS, GROUPS, GROUP)).reshape(GROUPS, BLOCK)

    gated = (grad_out.astype(F32) * gate[None, :]).astype(BF)
    gated = gated.reshape(TOK, SIDE, SIDE, SHARD).transpose(0, 2, 1, 3).reshape(TOK, SIDE * STRIP)
    gated_t = gated.T

    sent = call(
        second_payload,
        far((SIDE, STRIP + TOK, FEAT)),
        [col_spec, own],
        data=2 << 20,
        out_specs=anywhere,
        scratch_shapes=scratch(STRIP + TOK),
    )(kvw, queries)
    wq = swap(sent, ROW)

    sent = call(
        grad_payload,
        far((SIDE, FEAT, TOK)),
        [whole((TOK, SIDE * STRIP)), at((SIDE, STRIP, FEAT), (0, 0, 0))],
        flops=2 * TOK * FEAT * SIDE * STRIP,
        data=2 << 20,
        out_specs=anywhere,
        scratch_shapes=scratch(FEAT),
    )(gated, wq)
    grad_t = swap(sent, ROW)

    query_spec = at((SIDE, TOK, FEAT), (0, STRIP // TOK, 0))
    key_spec = at((SIDE, TOK, FEAT), (0, 0, 0))
    value_spec = at((SIDE, TOK, FEAT), (0, 1, 0))
    bias_spec = whole((GROUPS, BLOCK))
    stat_spec = whole((STATS, TOK))
    pair_count = HEADS_HERE * BLOCK * BLOCK
    half_spec = whole((FEAT, BLOCK))
    part, mean_key, part_lse = call(
        forward,
        (far((FEAT, BLOCK)), far((FEAT, BLOCK)), out((STATS, TOK), F32)),
        [query_spec, key_spec, value_spec, bias_spec],
        flops=24 * HD * pair_count,
        data=2 << 20,
        exps=pair_count,
    )(wq, kvw, kvw, bias)
    sent, part_delta = call(
        stats_payload,
        (far((SIDE, FEAT + 6 * STATS, TOK)), out((STATS, TOK), F32)),
        [half_spec, stat_spec, whole((SIDE, FEAT, TOK))],
        data=2 << 20,
    )(*hbm(part), part_lse, grad_t)
    parts = swap(sent, ROW)
    block_specs = [
        query_spec,
        key_spec,
        value_spec,
        whole((SIDE, FEAT, TOK)),
        bias_spec,
        stat_spec,
        stat_spec,
    ]
    query_share = call(
        query_grad,
        far((FEAT, BLOCK)),
        block_specs,
        flops=24 * HD * pair_count,
        data=3 << 20,
        exps=pair_count,
    )(wq, kvw, kvw, grad_t, bias, part_lse, part_delta)

    parts, query_share = lax.optimization_barrier((parts, query_share))
    lse, delta, attended = call(
        combine,
        (out((STATS, TOK), F32), out((STATS, TOK), F32), out((TOK, FEAT))),
        [pl.BlockSpec(memory_space=pltpu.SMEM), whole((SIDE, FEAT + 6 * STATS, TOK))],
        data=1 << 20,
        scratch_shapes=[pltpu.VMEM((SIDE, STATS, TOK), F32)],
    )(p.reshape(1).astype(jnp.int32), parts)
    scalar = pl.BlockSpec(memory_space=pltpu.SMEM)
    core = lax.axis_index("core").reshape(1).astype(jnp.int32)
    pair = lax.axis_index("yh").reshape(1).astype(jnp.int32)
    keep, send = call(
        branch_rows,
        (out((PAIRS, STRIP, TOK)), out((PAIRS, STRIP, TOK))),
        [scalar, own, at((SIDE, STRIP, FEAT), (0, 0, 0))],
        flops=2 * TOK * FEAT * SIDE * STRIP,
        data=2 << 20,
        scratch_shapes=[pltpu.VMEM((SIDE, STRIP, TOK), BF)],
    )(core, attended, wq)
    got = lax.ppermute(send, "core", [(0, 1), (1, 0)])
    chunks = call(
        add_halves,
        (out((STRIP, TOK)),) * PAIRS,
        [scalar] + [whole((PAIRS, STRIP, TOK))] * 2,
        data=2 << 20,
    )(pair, keep, got)

    sent_row = call(
        row_payload,
        far((SIDE, STRIP + TOK, FEAT)),
        [half_spec, half_spec] + [stat_spec] * 4 + [own, whole((SIDE * STRIP, TOK))],
        flops=2 * TOK * FEAT * SIDE * STRIP,
        data=3 << 20,
    )(*hbm(query_share, mean_key), part_lse, part_delta, lse, delta, attended, gated_t)
    got_row = swap(sent_row, ROW)
    got_row, chunks = lax.optimization_barrier((got_row, chunks))
    summed = [chunks[0]] + [
        lax.ppermute(chunks[d], "yh", [(i, (i + d) % PAIRS) for i in range(PAIRS)])
        for d in range(1, PAIRS)
    ]
    col_shape = (SIDE, 2 * TOK + SHARD, FEAT)
    sent_col = call(
        key_grads,
        far(col_shape),
        block_specs,
        flops=32 * HD * pair_count,
        data=3 << 20,
        exps=pair_count,
        scratch_shapes=[pltpu.VMEM((BLOCK, FEAT), F32)] * 2,
    )(wq, kvw, kvw, grad_t, bias, lse, delta)
    d_queries, sent_col = call(
        sum_first,
        (out((TOK, FEAT)), far(col_shape)),
        [row_spec, anywhere],
        data=2 << 20,
        out_specs=(own, anywhere),
        input_output_aliases={1: 1},
        scratch_shapes=[pltpu.VMEM((SIDE, SHARD, FEAT), BF), pltpu.SemaphoreType.DMA],
    )(got_row, sent_col)
    got_col = swap(sent_col, COL)
    d_keys, d_values, d_weight = call(
        sum_second,
        (out((TOK, FEAT)), out((TOK, FEAT)), out((SHARD, FEAT), F32)),
        [col_spec],
        data=1 << 20,
    )(got_col)

    col_count = residual.shape[1]
    gate_here = lax.dynamic_slice_in_dim(gate, lax.axis_index(FSDP) * col_count, col_count, 0)
    layer_out = call(
        finish,
        out((TOK, STRIP)),
        [whole((TOK, STRIP)), whole((1, STRIP))] + [whole((STRIP, TOK))] * PAIRS,
        data=1 << 20,
    )(*hbm(residual), gate_here[None, :], *summed)
    return (layer_out, d_queries, d_keys, d_values, d_weight.T)


def solution(mesh):
    fine = Mesh(mesh.devices.reshape(8, 4, 2, 4, 2), ("z", "x", "yl", "yh", "core"))
    seq = COL + ROW
    tile = P(seq, FSDP)
    in_specs = (tile, tile, tile, tile, P(), P(FSDP, seq), P(seq, None), P(), P())
    out_specs = (tile, tile, tile, tile, P(FSDP, seq))
    return jax.shard_map(local, mesh=fine, in_specs=in_specs, out_specs=out_specs, check_vma=False)
```

time: 149 us -> 127 us (0.85)
  the two profiles are of different devices: /device:TPU:17 before, /device:TPU:48 now
where the time goes in v2:
time: 127 us; the launch traced here: 126 us
  starting transfers between devices  34.3 us (27%)
  blocking collectives  29.9 us (24%)
  Pallas kernels  29.1 us (23%)
  waiting for transfers between devices  28.1 us (22%)
  local copies, waits for them, and re-layouts  1.86 us (1%)
    all_to_all x1, blocking collectives, swap(): return lax.all_to_all(a, axes, 0, 0, tiled=True)  29.9 us
    all_to_all x5, starting transfers between devices, swap(): return lax.all_to_all(a, axes, 0, 0, tiled=True)  20.7 us
    all_to_all x5, waiting for transfers between devices, swap(): return lax.all_to_all(a, axes, 0, 0, tiled=True)  20.4 us
    ppermute x3, starting transfers between devices, local(): lax.ppermute(chunks[d], 'yh', [(i, (i + d) % PAIRS) for i in range(PAIRS)])  11.5 us
    ppermute x3, waiting for transfers between devices, local(): lax.ppermute(chunks[d], 'yh', [(i, (i + d) % PAIRS) for i in range(PAIRS)])  7.64 us
    pallas_call x1, Pallas kernels, local(): call(forward, (far((FEAT, BLOCK)), far((FEAT, BLOCK)), out((STATS, TOK),...  6.45 us
    pallas_call x1, Pallas kernels, local(): call(key_grads, far(col_shape), block_specs, flops=32 * HD * pair_count,...  5.53 us
    pallas_call x1, Pallas kernels, local(): call(query_grad, far((FEAT, BLOCK)), block_specs, flops=24 * HD * pair_co...  4.28 us
  transfers between devices with their start and end apart: 9, of which 5 were waited for; matrix products, arithmetic and copies ran while one was open for 3% of the time, Pallas kernels for 15%

profile of v2, /device:TPU:48, one launch (start us, length us, event | category | flops | bytes accessed | tf_op | source)
XLA Modules:
  0.0 125.7 jit_solution(17174920771868293346)
XLA Ops:
  0.6 0.0 copy-start
  0.6 1.7 %shard_map.128 = bf16[8,304,128]{2,1,0:T(8,128)(2,1)} custom-call(bf16[128,128]{1,0:T(8,128)(2,1)} %k_ref.1, bf16[128,128]{1,0:T(8,128)(2,1)} %v_ref.1, bf16[48,128]{1,0:T(8,128)(2,1)} %bitcast.14), custom_call_target="tpu_custom_call" | custom-call | flops 1 | bytes 1048576 | tf_op jit(solution)/shard_map/pallas_call | solution.py:332
  2.4 29.9 %all_to_all.30.g_ref.k_ref.v_ref = bf16[8,304,128]{2,1,0:T(8,128)(2,1)S(1)} all-to-all(bf16[8,304,128]{2,1,0:T(8,128)(2,1)} %shard_map.128), channel_id=1, replica_groups=mesh['z'=8,'x'=4,'yl'=2,'yh'=4,'core'=2] {'z'}, dimensions={0} | all-to-all | bytes 1245184 | tf_op jit(solution)/shard_map/all_to_all | solution.py:70
  32.3 0.0 copy-done
  32.3 1.1 shard_map.129
  33.4 0.0 copy-start.3
  33.4 0.0 copy-start.1
  33.4 4.6 %all-to-all-start.1 = ((bf16[8,512,128]{2,1,0:T(8,128)(2,1)}), bf16[8,512,128]{2,1,0:T(8,128)(2,1)S(1)}, u32[]{:S(2)}, u32[]{:S(2)}) async-start(bf16[8,512,128]{2,1,0:T(8,128)(2,1)} %shard_map.129), calls=%async_computation.1 | async-start | bytes 2097152 | tf_op jit(solution)/shard_map/all_to_all | solution.py:70
  37.9 0.0 copy-start.2
  38.0 0.0 copy-done.3
  38.0 0.1 reshape.37
  38.1 0.1 eq.36
  38.2 0.6 eq.42
  38.8 0.0 copy-done.1
  38.8 0.4 copy.17
  39.2 0.0 copy-done.2
  39.2 0.5 multiply_convert_fusion
  39.7 0.1 copy.18
  39.7 0.3 copy.19.gated_ref
  40.0 0.0 copy-start.4
  40.0 12.3 %all-to-all-done.1.q_ref.w_ref = bf16[8,512,128]{2,1,0:T(8,128)(2,1)S(1)} async-done(((bf16[8,512,128]{2,1,0:T(8,128)(2,1)}), bf16[8,512,128]{2,1,0:T(8,128)(2,1)S(1)}, u32[]{:S(2)}, u32[]{:S(2)}) %all-to-all-start.1) | async-done | bytes 1048608 | tf_op jit(solution)/shard_map/all_to_all | solution.py:70
  52.4 1.3 shard_map.131
  53.6 3.4 %all-to-all-start.2 = ((bf16[8,128,128]{2,1,0:T(8,128)(2,1)}), bf16[8,128,128]{2,1,0:T(8,128)(2,1)S(1)}, u32[]{:S(2)}, u32[]{:S(2)}) async-start(bf16[8,128,128]{2,1,0:T(8,128)(2,1)} %shard_map.131), calls=%async_computation.2 | async-start | bytes 524288 | tf_op jit(solution)/shard_map/all_to_all | solution.py:70
  57.1 0.0 copy-done.4
  57.1 1.2 fusion.3
  58.2 0.1 broadcast_in_dim.23
  58.3 0.1 reshape.38.bias_ref
  58.5 6.5 %shard_map.130 = (bf16[128,1024]{1,0:T(8,128)(2,1)}, bf16[128,1024]{1,0:T(8,128)(2,1)}, f32[16,128]{1,0:T(8,128)S(1)}) custom-call(bf16[8,512,128]{2,1,0:T(8,128)(2,1)S(1)} %all-to-all-done.1.q_ref.w_ref, bf16[8,304,128]{2,1,0:T(8,128)(2,1)S(1)} %all_to_all.30.g_ref.k_ref.v_ref, bf16[8,304,128]{2,1,0:T(8,128)(2,1)S(1)} %all_to_all.30.g_ref.k_ref.v_ref, ...), custom_call_target="tpu_custom_call" | custom-call | flops 3221225472 | bytes 2097152 | tf_op jit(solution)/shard_map/pallas_call | solution.py:387
  64.9 0.0 all-to-all-done.2.grad_ref
  64.9 1.8 %shard_map.132 = (bf16[8,224,128]{2,1,0:T(8,128)(2,1)}, f32[16,128]{1,0:T(8,128)S(1)}) custom-call(bf16[128,1024]{1,0:T(8,128)(2,1)} %get-tuple-element.31.o_ref, f32[16,128]{1,0:T(8,128)S(1)} %get-tuple-element.32.lse_ref, bf16[8,128,128]{2,1,0:T(8,128)(2,1)S(1)} %all-to-all-done.2.grad_ref), custom_call_target="tpu_custom_call" | custom-call | flops 1 | bytes 2097152 | tf_op jit(solution)/shard_map/pallas_call | solution.py:395
  66.8 5.6 %all-to-all-start.3 = ((bf16[8,224,128]{2,1,0:T(8,128)(2,1)}), bf16[8,224,128]{2,1,0:T(8,128)(2,1)S(1)}, u32[]{:S(2)}, u32[]{:S(2)}) async-start(bf16[8,224,128]{2,1,0:T(8,128)(2,1)} %get-tuple-element.33), calls=%async_computation.3 | async-start | bytes 917504 | tf_op jit(solution)/shard_map/all_to_all | solution.py:70
  72.4 4.3 %shard_map.133.grad_ref = bf16[128,1024]{1,0:T(8,128)(2,1)} custom-call(bf16[8,512,128]{2,1,0:T(8,128)(2,1)S(1)} %all-to-all-done.1.q_ref.w_ref, bf16[8,304,128]{2,1,0:T(8,128)(2,1)S(1)} %all_to_all.30.g_ref.k_ref.v_ref, bf16[8,304,128]{2,1,0:T(8,128)(2,1)S(1)} %all_to_all.30.g_ref.k_ref.v_ref, bf16[8,128,128]{2,1,0:T(8,128)(2,1)S(1)} %all-to-all-done.2.grad_ref, ...), custom_call_target="tpu_custom_call" | custom-call | flops 3221225472 | bytes 3145728 | tf_op jit(solution)/shard_map/pallas_call | solution.py:411
  76.7 4.1 %all-to-all-done.3.d_ref = bf16[8,224,128]{2,1,0:T(8,128)(2,1)S(1)} async-done(((bf16[8,224,128]{2,1,0:T(8,128)(2,1)}), bf16[8,224,128]{2,1,0:T(8,128)(2,1)S(1)}, u32[]{:S(2)}, u32[]{:S(2)}) %all-to-all-start.3) | async-done | bytes 458784 | tf_op jit(solution)/shard_map/all_to_all | solution.py:70
  80.7 0.2 shard_map.134
  80.9 2.4 %shard_map.135 = bf16[8,512,128]{2,1,0:T(8,128)(2,1)} custom-call(bf16[128,1024]{1,0:T(8,128)(2,1)} %shard_map.133.grad_ref, bf16[128,1024]{1,0:T(8,128)(2,1)} %get-tuple-element.36.mean_ref, f32[16,128]{1,0:T(8,128)S(1)} %get-tuple-element.32.lse_ref, f32[16,128]{1,0:T(8,128)S(1)} %get-tuple-element.34.delta_ref, ...), custom_call_target="tpu_custom_call" | custom-call | flops 100663296 | bytes 3145728 | tf_op jit(solution)/shard_map/pallas_call | solution.py:447
  83.3 3.6 %all-to-all-start.4 = ((bf16[8,512,128]{2,1,0:T(8,128)(2,1)}), bf16[8,512,128]{2,1,0:T(8,128)(2,1)S(1)}, u32[]{:S(2)}, u32[]{:S(2)}) async-start(bf16[8,512,128]{2,1,0:T(8,128)(2,1)} %shard_map.135), calls=%async_computation.4 | async-start | bytes 2097152 | tf_op jit(solution)/shard_map/all_to_all | solution.py:70
  86.9 0.4 shard_map.136
  87.3 2.1 %collective-permute-start = (bf16[4,384,128]{2,1,0:T(8,128)(2,1)S(1)}, bf16[4,384,128]{2,1,0:T(8,128)(2,1)S(1)}, u32[]{:S(2)}, u32[]{:S(2)}) collective-permute-start(bf16[4,384,128]{2,1,0:T(8,128)(2,1)S(1)} %get-tuple-element.42), channel_id=1, source_target_pairs={{0,1},{1,0},{2,3},{3,2},{4,5},{5,4},{6,7},{7,6},{8,9},{9,8},{10,11... | collective-permute-start | bytes 1179656 | tf_op jit(solution)/shard_map/ppermute | solution.py:439
  89.4 5.5 %shard_map.139.f_in = bf16[8,304,128]{2,1,0:T(8,128)(2,1)} custom-call(bf16[8,512,128]{2,1,0:T(8,128)(2,1)S(1)} %all-to-all-done.1.q_ref.w_ref, bf16[8,304,128]{2,1,0:T(8,128)(2,1)S(1)} %all_to_all.30.g_ref.k_ref.v_ref, bf16[8,304,128]{2,1,0:T(8,128)(2,1)S(1)} %all_to_all.30.g_ref.k_ref.v_ref, bf16[8,128,128]{2,1,0:T(8,128)(2,1)S(1)} %all-to-all-done.2.grad_ref, ...), custom_call_target="tpu_custom_call" | custom-call | flops 4294967296 | bytes 3145728 | tf_op jit(solution)/shard_map/pallas_call | solution.py:461
  95.0 0.0 collective-permute-done.got_ref
  95.0 0.1 shard_map.137
  95.1 4.0 %all-to-all-done.4.e_ref = bf16[8,512,128]{2,1,0:T(8,128)(2,1)S(1)} async-done(((bf16[8,512,128]{2,1,0:T(8,128)(2,1)}), bf16[8,512,128]{2,1,0:T(8,128)(2,1)S(1)}, u32[]{:S(2)}, u32[]{:S(2)}) %all-to-all-start.4) | async-done | bytes 1048608 | tf_op jit(solution)/shard_map/all_to_all | solution.py:70
  99.1 1.4 %shard_map.140 = (bf16[128,128]{1,0:T(8,128)(2,1)}, bf16[8,304,128]{2,1,0:T(8,128)(2,1)}) custom-call(bf16[8,512,128]{2,1,0:T(8,128)(2,1)S(1)} %all-to-all-done.4.e_ref, bf16[8,304,128]{2,1,0:T(8,128)(2,1)} %shard_map.139.f_in), custom_call_target="tpu_custom_call", output_to_operand_aliasing={{1}: (1, {})} | custom-call | flops 1 | bytes 2097152 | tf_op jit(solution)/shard_map/pallas_call | solution.py:470
  100.5 3.6 %all-to-all-start.5 = ((bf16[8,304,128]{2,1,0:T(8,128)(2,1)}), bf16[8,304,128]{2,1,0:T(8,128)(2,1)S(1)}, u32[]{:S(2)}, u32[]{:S(2)}) async-start(bf16[8,304,128]{2,1,0:T(8,128)(2,1)} %get-tuple-element.53), calls=%async_computation.5 | async-start | bytes 1245184 | tf_op jit(solution)/shard_map/all_to_all | solution.py:70
  104.1 2.7 %collective-permute-start.1 = (bf16[384,128]{1,0:T(8,128)(2,1)S(1)}, bf16[384,128]{1,0:T(8,128)(2,1)S(1)}, u32[]{:S(2)}, u32[]{:S(2)}) collective-permute-start(bf16[384,128]{1,0:T(8,128)(2,1)S(1)} %get-tuple-element.48), channel_id=1, source_target_pairs={{0,2},{2,4},{4,6},{6,0},{1,3},{3,5},{5,7},{7,1},{8,10},{10,12},{12... | collective-permute-start | bytes 294920 | tf_op jit(solution)/shard_map/ppermute | solution.py:457
  106.8 6.8 %collective-permute-start.2 = (bf16[384,128]{1,0:T(8,128)(2,1)S(1)}, bf16[384,128]{1,0:T(8,128)(2,1)S(1)}, u32[]{:S(2)}, u32[]{:S(2)}) collective-permute-start(bf16[384,128]{1,0:T(8,128)(2,1)S(1)} %get-tuple-element.49), channel_id=1, source_target_pairs={{0,4},{2,6},{4,0},{6,2},{1,5},{3,7},{5,1},{7,3},{8,12},{10,14},{12... | collective-permute-start | bytes 294920 | tf_op jit(solution)/shard_map/ppermute | solution.py:457
  113.6 1.9 %collective-permute-start.3 = (bf16[384,128]{1,0:T(8,128)(2,1)S(1)}, bf16[384,128]{1,0:T(8,128)(2,1)S(1)}, u32[]{:S(2)}, u32[]{:S(2)}) collective-permute-start(bf16[384,128]{1,0:T(8,128)(2,1)S(1)} %get-tuple-element.50), channel_id=1, source_target_pairs={{0,6},{2,0},{4,2},{6,4},{1,7},{3,1},{5,3},{7,5},{8,14},{10,8},{12,... | collective-permute-start | bytes 294920 | tf_op jit(solution)/shard_map/ppermute | solution.py:457
  115.6 0.1 dynamic_slice.11
  115.7 0.0 collective-permute-done.1.refs_1_
  115.7 1.5 %collective-permute-done.2.refs_2_ = bf16[384,128]{1,0:T(8,128)(2,1)S(1)} collective-permute-done((bf16[384,128]{1,0:T(8,128)(2,1)S(1)}, bf16[384,128]{1,0:T(8,128)(2,1)S(1)}, u32[]{:S(2)}, u32[]{:S(2)}) %collective-permute-start.2) | collective-permute-done | bytes 98336 | tf_op jit(solution)/shard_map/ppermute | solution.py:457
  117.2 6.1 %collective-permute-done.3.refs_3_ = bf16[384,128]{1,0:T(8,128)(2,1)S(1)} collective-permute-done((bf16[384,128]{1,0:T(8,128)(2,1)S(1)}, bf16[384,128]{1,0:T(8,128)(2,1)S(1)}, u32[]{:S(2)}, u32[]{:S(2)}) %collective-permute-start.3) | collective-permute-done | bytes 98336 | tf_op jit(solution)/shard_map/ppermute | solution.py:457
  123.3 1.7 %shard_map.138 = bf16[128,384]{1,0:T(8,128)(2,1)} custom-call(bf16[128,384]{1,0:T(8,128)(2,1)} %residual_ref.1, f32[1,384]{1,0:T(1,128)S(1)} %broadcast_in_dim.20.gate_ref, bf16[384,128]{1,0:T(8,128)(2,1)S(1)} %get-tuple-element.47.refs_0_, bf16[384,128]{1,0:T(8,128)(2,1)S(1)} %collective-permute-done.1.refs_1_, ...), custom_call_target="tpu_custom_call" | custom-call | flops 1 | bytes 1048576 | tf_op jit(solution)/shard_map/pallas_call | solution.py:489
  125.0 0.0 all-to-all-done.5.f_ref
  125.0 0.7 shard_map.141
  (3 shorter events, 0.0 us)
Async XLA Ops:
  0.6 31.7 %copy-start = (bf16[128,128]{1,0:T(8,128)(2,1)S(1)}, bf16[128,128]{1,0:T(8,128)(2,1)}, u32[]{:S(2)}) copy-start(bf16[128,128]{1,0:T(8,128)(2,1)} %q_ref.1) | copy-start | bytes 98308
  33.4 4.6 %copy-start.3 = (s32[128]{0:T(128)S(1)}, s32[128]{0:T(128)}, u32[]{:S(2)}) copy-start(s32[128]{0:T(128)} %param.17) | copy-start | bytes 1540
  33.4 5.4 %copy-start.1 = (bf16[128,3072]{1,0:T(8,128)(2,1)S(1)}, bf16[128,3072]{1,0:T(8,128)(2,1)}, u32[]{:S(2)}) copy-start(bf16[128,3072]{1,0:T(8,128)(2,1)} %param.15) | copy-start | bytes 2359300
  33.4 19.0 %all-to-all-start.1 = ((bf16[8,512,128]{2,1,0:T(8,128)(2,1)}), bf16[8,512,128]{2,1,0:T(8,128)(2,1)S(1)}, u32[]{:S(2)}, u32[]{:S(2)}) async-start(bf16[8,512,128]{2,1,0:T(8,128)(2,1)} %shard_map.129), calls=%async_computation.1 | async-start | bytes 2097152 | tf_op jit(solution)/shard_map/all_to_all | solution.py:70
  37.9 1.2 copy-start.2
  40.0 17.0 %copy-start.4 = (s32[16]{0:T(128)S(1)}, s32[16]{0:T(128)}, u32[]{:S(2)}) copy-start(s32[16]{0:T(128)} %eq.42) | copy-start | bytes 196
  53.6 11.3 %all-to-all-start.2 = ((bf16[8,128,128]{2,1,0:T(8,128)(2,1)}), bf16[8,128,128]{2,1,0:T(8,128)(2,1)S(1)}, u32[]{:S(2)}, u32[]{:S(2)}) async-start(bf16[8,128,128]{2,1,0:T(8,128)(2,1)} %shard_map.131), calls=%async_computation.2 | async-start | bytes 524288 | tf_op jit(solution)/shard_map/all_to_all | solution.py:70
  66.8 14.0 %all-to-all-start.3 = ((bf16[8,224,128]{2,1,0:T(8,128)(2,1)}), bf16[8,224,128]{2,1,0:T(8,128)(2,1)S(1)}, u32[]{:S(2)}, u32[]{:S(2)}) async-start(bf16[8,224,128]{2,1,0:T(8,128)(2,1)} %get-tuple-element.33), calls=%async_computation.3 | async-start | bytes 917504 | tf_op jit(solution)/shard_map/all_to_all | solution.py:70
  83.3 15.8 %all-to-all-start.4 = ((bf16[8,512,128]{2,1,0:T(8,128)(2,1)}), bf16[8,512,128]{2,1,0:T(8,128)(2,1)S(1)}, u32[]{:S(2)}, u32[]{:S(2)}) async-start(bf16[8,512,128]{2,1,0:T(8,128)(2,1)} %shard_map.135), calls=%async_computation.4 | async-start | bytes 2097152 | tf_op jit(solution)/shard_map/all_to_all | solution.py:70
  87.3 7.6 %collective-permute-start = (bf16[4,384,128]{2,1,0:T(8,128)(2,1)S(1)}, bf16[4,384,128]{2,1,0:T(8,128)(2,1)S(1)}, u32[]{:S(2)}, u32[]{:S(2)}) collective-permute-start(bf16[4,384,128]{2,1,0:T(8,128)(2,1)S(1)} %get-tuple-element.42), channel_id=1, source_target_pairs={{0,1},{1,0},{2,3},{3,2},{4,5},{5,4},{6,7},{7,6},{8,9},{9,8},{10,11... | collective-permute-start | bytes 1179656 | tf_op jit(solution)/shard_map/ppermute | solution.py:439
  100.5 24.5 %all-to-all-start.5 = ((bf16[8,304,128]{2,1,0:T(8,128)(2,1)}), bf16[8,304,128]{2,1,0:T(8,128)(2,1)S(1)}, u32[]{:S(2)}, u32[]{:S(2)}) async-start(bf16[8,304,128]{2,1,0:T(8,128)(2,1)} %get-tuple-element.53), calls=%async_computation.5 | async-start | bytes 1245184 | tf_op jit(solution)/shard_map/all_to_all | solution.py:70
  104.1 11.6 %collective-permute-start.1 = (bf16[384,128]{1,0:T(8,128)(2,1)S(1)}, bf16[384,128]{1,0:T(8,128)(2,1)S(1)}, u32[]{:S(2)}, u32[]{:S(2)}) collective-permute-start(bf16[384,128]{1,0:T(8,128)(2,1)S(1)} %get-tuple-element.48), channel_id=1, source_target_pairs={{0,2},{2,4},{4,6},{6,0},{1,3},{3,5},{5,7},{7,1},{8,10},{10,12},{12... | collective-permute-start | bytes 294920 | tf_op jit(solution)/shard_map/ppermute | solution.py:457
  106.8 10.4 %collective-permute-start.2 = (bf16[384,128]{1,0:T(8,128)(2,1)S(1)}, bf16[384,128]{1,0:T(8,128)(2,1)S(1)}, u32[]{:S(2)}, u32[]{:S(2)}) collective-permute-start(bf16[384,128]{1,0:T(8,128)(2,1)S(1)} %get-tuple-element.49), channel_id=1, source_target_pairs={{0,4},{2,6},{4,0},{6,2},{1,5},{3,7},{5,1},{7,3},{8,12},{10,14},{12... | collective-permute-start | bytes 294920 | tf_op jit(solution)/shard_map/ppermute | solution.py:457
  113.6 9.7 %collective-permute-start.3 = (bf16[384,128]{1,0:T(8,128)(2,1)S(1)}, bf16[384,128]{1,0:T(8,128)(2,1)S(1)}, u32[]{:S(2)}, u32[]{:S(2)}) collective-permute-start(bf16[384,128]{1,0:T(8,128)(2,1)S(1)} %get-tuple-element.50), channel_id=1, source_target_pairs={{0,6},{2,0},{4,2},{6,4},{1,7},{3,1},{5,3},{7,5},{8,14},{10,8},{12,... | collective-permute-start | bytes 294920 | tf_op jit(solution)/shard_map/ppermute | solution.py:457

commit v3 on v2

--- a/solution.py
+++ b/solution.py
@@ -19,7 +19,8 @@
 GROUPS = BLOCK // GROUP
 SHARD = 48
 STRIP = SIDE * SHARD
-TILE = 256
+QUERY_TILE = 512
+KEY_TILE = 256
 MASKED = -1e30
 STATS = HEADS_HERE * SIDE
 VMEM = 32 * 1024 * 1024
@@ -116,9 +117,9 @@
     return a.astype(F32).T.astype(BF)
 
 
-def row_of(ref, head, tile):
-    first = head * SIDE + tile * (TILE // TOK)
-    return jnp.concatenate([ref[first + c : first + c + 1, :] for c in range(TILE // TOK)], axis=1)
+def row_of(ref, head, first=0, count=SIDE):
+    rows = range(head * SIDE + first, head * SIDE + first + count)
+    return jnp.concatenate([ref[i : i + 1, :] for i in rows], axis=1)
 
 
 def forward(q_ref, k_ref, v_ref, bias_ref, o_ref, mean_ref, lse_ref):
@@ -129,21 +130,18 @@
     v_t = transposed(v_ref[...].reshape(BLOCK, FEAT))
     for head in range(HEADS_HERE):
         rows = slice(head * HD, (head + 1) * HD)
-        q_op = query_operand(q_t, bias_ref[...], head)
+        s = mm(k_op, query_operand(q_t, bias_ref[...], head))
+        top = jnp.max(s, axis=0, keepdims=True)
+        p = jnp.exp(s - top)
+        total = jnp.sum(p, axis=0, keepdims=True)
         both = jnp.concatenate([v_t[rows], k_t[rows]], axis=0)
-        for tile in range(BLOCK // TILE):
-            span = slice(tile * TILE, (tile + 1) * TILE)
-            s = mm(k_op, q_op[:, span])
-            top = jnp.max(s, axis=0, keepdims=True)
-            p = jnp.exp(s - top)
-            total = jnp.sum(p, axis=0, keepdims=True)
-            part = mm(both, p.astype(BF)) * (1.0 / total)
-            o_ref[rows, span] = part[:HD].astype(BF)
-            mean_ref[rows, span] = part[HD:].astype(BF)
-            lse = top + jnp.log(total)
-            for c in range(TILE // TOK):
-                row = head * SIDE + tile * (TILE // TOK) + c
-                lse_ref[row : row + 1, :] = lse[:, c * TOK : (c + 1) * TOK]
+        part = mm(both, p.astype(BF)) * (1.0 / total)
+        o_ref[rows] = part[:HD].astype(BF)
+        mean_ref[rows] = part[HD:].astype(BF)
+        lse = top + jnp.log(total)
+        for c in range(SIDE):
+            row = head * SIDE + c
+            lse_ref[row : row + 1, :] = lse[:, c * TOK : (c + 1) * TOK]
 
 
 def split3(a):
@@ -180,10 +178,11 @@
         rows = slice(head * HD, (head + 1) * HD)
         q_op = query_operand(q_t, bias_ref[...], head)
         grad_op = jnp.where(feat_row == head, grad_t.astype(F32), 0.0).astype(BF)
-        for tile in range(BLOCK // TILE):
-            span = slice(tile * TILE, (tile + 1) * TILE)
-            p = jnp.exp(mm(k_op, q_op[:, span]) - row_of(lse_ref, head, tile))
-            ds = (p * (mm(v, grad_op[:, span]) - row_of(delta_ref, head, tile))).astype(BF)
+        for tile in range(BLOCK // QUERY_TILE):
+            span = slice(tile * QUERY_TILE, (tile + 1) * QUERY_TILE)
+            part = (head, tile * (QUERY_TILE // TOK), QUERY_TILE // TOK)
+            p = jnp.exp(mm(k_op, q_op[:, span]) - row_of(lse_ref, *part))
+            ds = (p * (mm(v, grad_op[:, span]) - row_of(delta_ref, *part))).astype(BF)
             o_ref[rows, span] = mm(k_t[rows], ds).astype(BF)
 
 
@@ -220,7 +219,7 @@
     att_ref[...] = jnp.concatenate(heads, axis=0).T.astype(BF)
 
 
-def branch_rows(core_ref, att_ref, w_ref, keep_ref, send_ref, all_ref):
+def branch_rows(place_ref, att_ref, w_ref, keep_ref, send_ref, all_ref):
     att = att_ref[...]
     for i in range(SIDE):
         part = lax.dot_general(
@@ -228,22 +227,30 @@
         ).astype(BF)
         for j in range(SIDE):
             all_ref[j, i * SHARD : (i + 1) * SHARD] = part[j * SHARD : (j + 1) * SHARD]
-    core = core_ref[0]
+    core = place_ref[1]
     for i in range(PAIRS):
         keep_ref[i] = all_ref[2 * i + core]
         send_ref[i] = all_ref[2 * i + 1 - core]
 
 
-def add_halves(pair_ref, keep_ref, got_ref, *out_refs):
-    for d, o_ref in enumerate(out_refs):
-        i = lax.rem(pair_ref[0] + d, PAIRS)
-        o_ref[...] = (keep_ref[i].astype(F32) + got_ref[i].astype(F32)).astype(BF)
+def add_halves(place_ref, keep_ref, got_ref, own_ref, far_ref, ahead_ref, behind_ref):
+    pair, ahead = place_ref[0], 1 - 2 * place_ref[1]
+    steps = ((own_ref, 0), (far_ref, 2), (ahead_ref, ahead), (behind_ref, -ahead))
+    for ref, step in steps:
+        i = lax.rem(pair + step + PAIRS, PAIRS)
+        ref[...] = (keep_ref[i].astype(F32) + got_ref[i].astype(F32)).astype(BF)
+
+
+def relay(ahead_ref, got_ref, o_ref):
+    o_ref[...] = (ahead_ref[...].astype(F32) + got_ref[...].astype(F32)).astype(BF)
 
 
 def row_payload(
-    grad_ref, mean_ref, lse_ref, delta_ref, all_lse_ref, all_delta_ref, att_ref, gated_ref, e_ref
+    grad_ref, mean_ref, lse_ref, delta_ref, all_lse_ref, all_delta_ref, att_ref, gated_ref, o_ref,
+    e_ref, sems,
 ):
     att = att_ref[...]
+    copies = []
     for i in range(SIDE):
         cols = slice(i * TOK, (i + 1) * TOK)
         for head in range(HEADS_HERE):
@@ -254,6 +261,10 @@
             part = grad_ref[rows, cols].astype(F32) - shift * mean_ref[rows, cols].astype(F32)
             e_ref[i, STRIP + head * HD : STRIP + (head + 1) * HD] = (weight * part).astype(BF)
         e_ref[i, 0:STRIP] = mm(gated_ref[i * STRIP : (i + 1) * STRIP], att).astype(BF)
+        copies.append(pltpu.make_async_copy(e_ref.at[i], o_ref.at[i], sems.at[i]))
+        copies[i].start()
+    for copy in copies:
+        copy.wait()
 
 
 def key_grads(
@@ -275,10 +286,11 @@
         grad_op = jnp.where(feat_row == head, grad_t.astype(F32), 0.0).astype(BF)
         q_rows = jnp.where(feat_col == head, q.astype(F32), 0.0).astype(BF)
         grad_rows = jnp.where(feat_col == head, grad.astype(F32), 0.0).astype(BF)
-        for tile in range(BLOCK // TILE):
-            span = slice(tile * TILE, (tile + 1) * TILE)
-            p = jnp.exp(mm(k_op, q_op[:, span]) - row_of(lse_ref, head, tile))
-            ds = (p * (mm(v, grad_op[:, span]) - row_of(delta_ref, head, tile))).astype(BF)
+        for tile in range(BLOCK // KEY_TILE):
+            span = slice(tile * KEY_TILE, (tile + 1) * KEY_TILE)
+            part = (head, tile * (KEY_TILE // TOK), KEY_TILE // TOK)
+            p = jnp.exp(mm(k_op, q_op[:, span]) - row_of(lse_ref, *part))
+            ds = (p * (mm(v, grad_op[:, span]) - row_of(delta_ref, *part))).astype(BF)
             dv_ref[...] += mm(p.astype(BF), grad_rows[span])
             dk_ref[...] += mm(ds, q_rows[span])
     for i in range(SIDE):
@@ -366,6 +378,7 @@
     )(kvw, queries)
     wq = swap(sent, ROW)
 
+    gated, wq, bias = lax.optimization_barrier((gated, wq, bias))
     sent = call(
         grad_payload,
         far((SIDE, FEAT, TOK)),
@@ -426,8 +439,7 @@
         scratch_shapes=[pltpu.VMEM((SIDE, STATS, TOK), F32)],
     )(p.reshape(1).astype(jnp.int32), parts)
     scalar = pl.BlockSpec(memory_space=pltpu.SMEM)
-    core = lax.axis_index("core").reshape(1).astype(jnp.int32)
-    pair = lax.axis_index("yh").reshape(1).astype(jnp.int32)
+    place = jnp.stack([lax.axis_index("yh"), lax.axis_index("core")]).astype(jnp.int32)
     keep, send = call(
         branch_rows,
         (out((PAIRS, STRIP, TOK)), out((PAIRS, STRIP, TOK))),
@@ -435,14 +447,14 @@
         flops=2 * TOK * FEAT * SIDE * STRIP,
         data=2 << 20,
         scratch_shapes=[pltpu.VMEM((SIDE, STRIP, TOK), BF)],
-    )(core, attended, wq)
+    )(place, attended, wq)
     got = lax.ppermute(send, "core", [(0, 1), (1, 0)])
     chunks = call(
         add_halves,
         (out((STRIP, TOK)),) * PAIRS,
         [scalar] + [whole((PAIRS, STRIP, TOK))] * 2,
         data=2 << 20,
-    )(pair, keep, got)
+    )(place, keep, got)
 
     sent_row = call(
         row_payload,
@@ -450,13 +462,30 @@
         [half_spec, half_spec] + [stat_spec] * 4 + [own, whole((SIDE * STRIP, TOK))],
         flops=2 * TOK * FEAT * SIDE * STRIP,
         data=3 << 20,
+        out_specs=anywhere,
+        scratch_shapes=[
+            pltpu.VMEM((SIDE, STRIP + TOK, FEAT), BF),
+            pltpu.SemaphoreType.DMA((SIDE,)),
+        ],
     )(*hbm(query_share, mean_key), part_lse, part_delta, lse, delta, attended, gated_t)
     got_row = swap(sent_row, ROW)
     got_row, chunks = lax.optimization_barrier((got_row, chunks))
-    summed = [chunks[0]] + [
-        lax.ppermute(chunks[d], "yh", [(i, (i + d) % PAIRS) for i in range(PAIRS)])
-        for d in range(1, PAIRS)
-    ]
+    mine, far_chunk, ahead_chunk, behind_chunk = chunks
+
+    def pass_on(a, step):
+        pairs = [
+            (2 * i + c, 2 * ((i + step * (1 - 2 * c)) % PAIRS) + c)
+            for i in range(PAIRS)
+            for c in range(2)
+        ]
+        return lax.ppermute(a, FSDP, pairs)
+
+    strip_spec = whole((STRIP, TOK))
+    from_ahead = pass_on(behind_chunk, -1)
+    ahead_chunk = call(relay, out((STRIP, TOK)), [strip_spec, strip_spec], data=1 << 18)(
+        ahead_chunk, pass_on(far_chunk, 1)
+    )
+    summed = (mine, from_ahead, pass_on(ahead_chunk, 1))
     col_shape = (SIDE, 2 * TOK + SHARD, FEAT)
     sent_col = call(
         key_grads,
@@ -489,9 +518,9 @@
     layer_out = call(
         finish,
         out((TOK, STRIP)),
-        [whole((TOK, STRIP)), whole((1, STRIP))] + [whole((STRIP, TOK))] * PAIRS,
+        [whole((TOK, STRIP)), whole((1, STRIP))] + [strip_spec] * 3,
         data=1 << 20,
-    )(*hbm(residual), gate_here[None, :], *summed)
+    )(residual, gate_here[None, :], *summed)
     return (layer_out, d_queries, d_keys, d_values, d_weight.T)
 
 

time: 127 us -> 124 us (0.976)
  the two profiles are of different devices: /device:TPU:48 before, /device:TPU:64 now
where the time goes in v3:
time: 124 us; the launch traced here: 123 us
  starting transfers between devices  36.5 us (29%)
  waiting for transfers between devices  28.4 us (23%)
  blocking collectives  28.1 us (23%)
  Pallas kernels  26.7 us (22%)
  local copies, waits for them, and re-layouts  1.35 us (1%)
    all_to_all x1, blocking collectives, swap(): return lax.all_to_all(a, axes, 0, 0, tiled=True)  28.1 us
    all_to_all x5, starting transfers between devices, swap(): return lax.all_to_all(a, axes, 0, 0, tiled=True)  22.7 us
    all_to_all x5, waiting for transfers between devices, swap(): return lax.all_to_all(a, axes, 0, 0, tiled=True)  20.7 us
    ppermute x3, starting transfers between devices, pass_on(): return lax.ppermute(a, FSDP, pairs)  11.8 us
    ppermute x3, waiting for transfers between devices, pass_on(): return lax.ppermute(a, FSDP, pairs)  7.7 us
    pallas_call x1, Pallas kernels, local(): call(key_grads, far(col_shape), block_specs, flops=32 * HD * pair_count,...  5.54 us
    pallas_call x1, Pallas kernels, local(): call(forward, (far((FEAT, BLOCK)), far((FEAT, BLOCK)), out((STATS, TOK),...  4.28 us
    pallas_call x1, Pallas kernels, local(): call(query_grad, far((FEAT, BLOCK)), block_specs, flops=24 * HD * pair_co...  3.95 us
  transfers between devices with their start and end apart: 9, of which 7 were waited for; matrix products, arithmetic and copies ran while one was open for 2% of the time, Pallas kernels for 13%

profile of v3, /device:TPU:64, one launch (start us, length us, event | category | flops | bytes accessed | tf_op | source)
XLA Modules:
  0.0 122.8 jit_solution(12733970010602840890)
XLA Ops:
  0.6 0.0 copy-start.1
  0.6 1.7 %shard_map.128 = bf16[8,304,128]{2,1,0:T(8,128)(2,1)} custom-call(bf16[128,128]{1,0:T(8,128)(2,1)} %k_ref.1, bf16[128,128]{1,0:T(8,128)(2,1)} %v_ref.1, bf16[48,128]{1,0:T(8,128)(2,1)} %bitcast.14), custom_call_target="tpu_custom_call" | custom-call | flops 1 | bytes 1048576 | tf_op jit(solution)/shard_map/pallas_call | solution.py:344
  2.4 28.1 %all_to_all.30.g_ref.k_ref.v_ref = bf16[8,304,128]{2,1,0:T(8,128)(2,1)S(1)} all-to-all(bf16[8,304,128]{2,1,0:T(8,128)(2,1)} %shard_map.128), channel_id=1, replica_groups=mesh['z'=8,'x'=4,'yl'=2,'yh'=4,'core'=2] {'z'}, dimensions={0} | all-to-all | bytes 1245184 | tf_op jit(solution)/shard_map/all_to_all | solution.py:71
  30.5 0.0 copy-done.1
  30.5 1.1 shard_map.129
  31.6 0.0 copy-start.4
  31.6 0.0 copy-start.5
  31.6 0.0 copy-start.2
  31.6 5.5 %all-to-all-start.1 = ((bf16[8,512,128]{2,1,0:T(8,128)(2,1)}), bf16[8,512,128]{2,1,0:T(8,128)(2,1)S(1)}, u32[]{:S(2)}, u32[]{:S(2)}) async-start(bf16[8,512,128]{2,1,0:T(8,128)(2,1)} %shard_map.129), calls=%async_computation.1 | async-start | bytes 2097152 | tf_op jit(solution)/shard_map/all_to_all | solution.py:71
  37.1 0.0 copy-start.3
  37.1 0.0 copy-done.4
  37.1 0.1 reshape.33
  37.3 0.1 eq.36
  37.3 0.1 eq.42
  37.4 0.0 copy-done.5
  37.4 0.3 fusion.3
  37.7 0.1 broadcast_in_dim.23
  37.9 0.1 reshape.34.bias_ref
  38.0 0.0 copy-done.2
  38.0 0.4 copy.17
  38.4 0.0 copy-done.3
  38.4 0.5 multiply_convert_fusion
  38.8 0.1 copy.18
  38.9 11.3 %all-to-all-done.1.q_ref.w_ref = bf16[8,512,128]{2,1,0:T(8,128)(2,1)S(1)} async-done(((bf16[8,512,128]{2,1,0:T(8,128)(2,1)}), bf16[8,512,128]{2,1,0:T(8,128)(2,1)S(1)}, u32[]{:S(2)}, u32[]{:S(2)}) %all-to-all-start.1) | async-done | bytes 1048608 | tf_op jit(solution)/shard_map/all_to_all | solution.py:71
  50.2 0.3 copy.19.gated_ref
  50.5 1.2 %shard_map.131 = bf16[8,128,128]{2,1,0:T(8,128)(2,1)} custom-call(bf16[128,3072]{1,0:T(8,128)(2,1)S(1)} %copy.19.gated_ref, bf16[8,512,128]{2,1,0:T(8,128)(2,1)S(1)} %all-to-all-done.1.q_ref.w_ref), custom_call_target="tpu_custom_call" | custom-call | flops 100663296 | bytes 2097152 | tf_op jit(solution)/shard_map/pallas_call | solution.py:382
  51.7 3.4 %all-to-all-start.2 = ((bf16[8,128,128]{2,1,0:T(8,128)(2,1)}), bf16[8,128,128]{2,1,0:T(8,128)(2,1)S(1)}, u32[]{:S(2)}, u32[]{:S(2)}) async-start(bf16[8,128,128]{2,1,0:T(8,128)(2,1)} %shard_map.131), calls=%async_computation.2 | async-start | bytes 524288 | tf_op jit(solution)/shard_map/all_to_all | solution.py:71
  55.2 4.3 %shard_map.130 = (bf16[128,1024]{1,0:T(8,128)(2,1)}, bf16[128,1024]{1,0:T(8,128)(2,1)}, f32[16,128]{1,0:T(8,128)S(1)}) custom-call(bf16[8,512,128]{2,1,0:T(8,128)(2,1)S(1)} %all-to-all-done.1.q_ref.w_ref, bf16[8,304,128]{2,1,0:T(8,128)(2,1)S(1)} %all_to_all.30.g_ref.k_ref.v_ref, bf16[8,304,128]{2,1,0:T(8,128)(2,1)S(1)} %all_to_all.30.g_ref.k_ref.v_ref, ...), custom_call_target="tpu_custom_call" | custom-call | flops 3221225472 | bytes 2097152 | tf_op jit(solution)/shard_map/pallas_call | solution.py:400
  59.4 2.9 %all-to-all-done.2.grad_ref = bf16[8,128,128]{2,1,0:T(8,128)(2,1)S(1)} async-done(((bf16[8,128,128]{2,1,0:T(8,128)(2,1)}), bf16[8,128,128]{2,1,0:T(8,128)(2,1)S(1)}, u32[]{:S(2)}, u32[]{:S(2)}) %all-to-all-start.2) | async-done | bytes 262176 | tf_op jit(solution)/shard_map/all_to_all | solution.py:71
  62.4 1.8 %shard_map.132 = (bf16[8,224,128]{2,1,0:T(8,128)(2,1)}, f32[16,128]{1,0:T(8,128)S(1)}) custom-call(bf16[128,1024]{1,0:T(8,128)(2,1)} %get-tuple-element.36.o_ref, f32[16,128]{1,0:T(8,128)S(1)} %get-tuple-element.37.lse_ref, bf16[8,128,128]{2,1,0:T(8,128)(2,1)S(1)} %all-to-all-done.2.grad_ref), custom_call_target="tpu_custom_call" | custom-call | flops 1 | bytes 2097152 | tf_op jit(solution)/shard_map/pallas_call | solution.py:408
  64.2 3.5 %all-to-all-start.3 = ((bf16[8,224,128]{2,1,0:T(8,128)(2,1)}), bf16[8,224,128]{2,1,0:T(8,128)(2,1)S(1)}, u32[]{:S(2)}, u32[]{:S(2)}) async-start(bf16[8,224,128]{2,1,0:T(8,128)(2,1)} %get-tuple-element.39), calls=%async_computation.3 | async-start | bytes 917504 | tf_op jit(solution)/shard_map/all_to_all | solution.py:71
  67.7 4.0 %shard_map.133.grad_ref = bf16[128,1024]{1,0:T(8,128)(2,1)} custom-call(bf16[8,512,128]{2,1,0:T(8,128)(2,1)S(1)} %all-to-all-done.1.q_ref.w_ref, bf16[8,304,128]{2,1,0:T(8,128)(2,1)S(1)} %all_to_all.30.g_ref.k_ref.v_ref, bf16[8,304,128]{2,1,0:T(8,128)(2,1)S(1)} %all_to_all.30.g_ref.k_ref.v_ref, bf16[8,128,128]{2,1,0:T(8,128)(2,1)S(1)} %all-to-all-done.2.grad_ref, ...), custom_call_target="tpu_custom_call" | custom-call | flops 3221225472 | bytes 3145728 | tf_op jit(solution)/shard_map/pallas_call | solution.py:424
  71.7 4.3 %all-to-all-done.3.d_ref = bf16[8,224,128]{2,1,0:T(8,128)(2,1)S(1)} async-done(((bf16[8,224,128]{2,1,0:T(8,128)(2,1)}), bf16[8,224,128]{2,1,0:T(8,128)(2,1)S(1)}, u32[]{:S(2)}, u32[]{:S(2)}) %all-to-all-start.3) | async-done | bytes 458784 | tf_op jit(solution)/shard_map/all_to_all | solution.py:71
  76.0 0.2 shard_map.134
  76.2 2.3 %shard_map.135 = bf16[8,512,128]{2,1,0:T(8,128)(2,1)} custom-call(bf16[128,1024]{1,0:T(8,128)(2,1)} %shard_map.133.grad_ref, bf16[128,1024]{1,0:T(8,128)(2,1)} %get-tuple-element.42.mean_ref, f32[16,128]{1,0:T(8,128)S(1)} %get-tuple-element.37.lse_ref, f32[16,128]{1,0:T(8,128)S(1)} %get-tuple-element.40.delta_ref, ...), custom_call_target="tpu_custom_call" | custom-call | flops 100663296 | bytes 3145728 | tf_op jit(solution)/shard_map/pallas_call | solution.py:459
  78.5 3.6 %all-to-all-start.4 = ((bf16[8,512,128]{2,1,0:T(8,128)(2,1)}), bf16[8,512,128]{2,1,0:T(8,128)(2,1)S(1)}, u32[]{:S(2)}, u32[]{:S(2)}) async-start(bf16[8,512,128]{2,1,0:T(8,128)(2,1)} %shard_map.135), calls=%async_computation.4 | async-start | bytes 2097152 | tf_op jit(solution)/shard_map/all_to_all | solution.py:71
  82.0 0.1 pad_add_fusion.place_ref
  82.1 1.0 shard_map.136
  83.1 2.1 %collective-permute-start = (bf16[4,384,128]{2,1,0:T(8,128)(2,1)S(1)}, bf16[4,384,128]{2,1,0:T(8,128)(2,1)S(1)}, u32[]{:S(2)}, u32[]{:S(2)}) collective-permute-start(bf16[4,384,128]{2,1,0:T(8,128)(2,1)S(1)} %get-tuple-element.48), channel_id=1, source_target_pairs={{0,1},{1,0},{2,3},{3,2},{4,5},{5,4},{6,7},{7,6},{8,9},{9,8},{10,11... | collective-permute-start | bytes 1179656 | tf_op jit(solution)/shard_map/ppermute | solution.py:451
  85.2 5.5 %shard_map.140.f_in = bf16[8,304,128]{2,1,0:T(8,128)(2,1)} custom-call(bf16[8,512,128]{2,1,0:T(8,128)(2,1)S(1)} %all-to-all-done.1.q_ref.w_ref, bf16[8,304,128]{2,1,0:T(8,128)(2,1)S(1)} %all_to_all.30.g_ref.k_ref.v_ref, bf16[8,304,128]{2,1,0:T(8,128)(2,1)S(1)} %all_to_all.30.g_ref.k_ref.v_ref, bf16[8,128,128]{2,1,0:T(8,128)(2,1)S(1)} %all-to-all-done.2.grad_ref, ...), custom_call_target="tpu_custom_call" | custom-call | flops 4294967296 | bytes 3145728 | tf_op jit(solution)/shard_map/pallas_call | solution.py:490
  90.7 0.0 collective-permute-done.got_ref
  90.7 0.6 shard_map.137
  91.4 2.1 %all-to-all-done.4.e_ref = bf16[8,512,128]{2,1,0:T(8,128)(2,1)S(1)} async-done(((bf16[8,512,128]{2,1,0:T(8,128)(2,1)}), bf16[8,512,128]{2,1,0:T(8,128)(2,1)S(1)}, u32[]{:S(2)}, u32[]{:S(2)}) %all-to-all-start.4) | async-done | bytes 1048608 | tf_op jit(solution)/shard_map/all_to_all | solution.py:71
  93.5 1.4 %shard_map.141 = (bf16[128,128]{1,0:T(8,128)(2,1)}, bf16[8,304,128]{2,1,0:T(8,128)(2,1)}) custom-call(bf16[8,512,128]{2,1,0:T(8,128)(2,1)S(1)} %all-to-all-done.4.e_ref, bf16[8,304,128]{2,1,0:T(8,128)(2,1)} %shard_map.140.f_in), custom_call_target="tpu_custom_call", output_to_operand_aliasing={{1}: (1, {})} | custom-call | flops 1 | bytes 2097152 | tf_op jit(solution)/shard_map/pallas_call | solution.py:499
  95.0 0.0 copy-start
  95.0 6.7 %all-to-all-start.5 = ((bf16[8,304,128]{2,1,0:T(8,128)(2,1)}), bf16[8,304,128]{2,1,0:T(8,128)(2,1)S(1)}, u32[]{:S(2)}, u32[]{:S(2)}) async-start(bf16[8,304,128]{2,1,0:T(8,128)(2,1)} %get-tuple-element.59), calls=%async_computation.5 | async-start | bytes 1245184 | tf_op jit(solution)/shard_map/all_to_all | solution.py:71
  101.7 4.5 %collective-permute-start.2 = (bf16[384,128]{1,0:T(8,128)(2,1)S(1)}, bf16[384,128]{1,0:T(8,128)(2,1)S(1)}, u32[]{:S(2)}, u32[]{:S(2)}) collective-permute-start(bf16[384,128]{1,0:T(8,128)(2,1)S(1)} %get-tuple-element.56), channel_id=1, source_target_pairs={{0,2},{1,7},{2,4},{3,1},{4,6},{5,3},{6,0},{7,5},{8,10},{9,15},{10,... | collective-permute-start | bytes 294920 | tf_op jit(solution)/shard_map/ppermute | solution.py:481
  106.2 3.4 %collective-permute-start.1 = (bf16[384,128]{1,0:T(8,128)(2,1)S(1)}, bf16[384,128]{1,0:T(8,128)(2,1)S(1)}, u32[]{:S(2)}, u32[]{:S(2)}) collective-permute-start(bf16[384,128]{1,0:T(8,128)(2,1)S(1)} %get-tuple-element.54), channel_id=1, source_target_pairs={{0,6},{1,3},{2,0},{3,5},{4,2},{5,7},{6,4},{7,1},{8,14},{9,11},{10,... | collective-permute-start | bytes 294920 | tf_op jit(solution)/shard_map/ppermute | solution.py:481
  109.7 2.0 %collective-permute-done.2.got_ref = bf16[384,128]{1,0:T(8,128)(2,1)S(1)} collective-permute-done((bf16[384,128]{1,0:T(8,128)(2,1)S(1)}, bf16[384,128]{1,0:T(8,128)(2,1)S(1)}, u32[]{:S(2)}, u32[]{:S(2)}) %collective-permute-start.2) | collective-permute-done | bytes 98336 | tf_op jit(solution)/shard_map/ppermute | solution.py:481
  111.7 3.8 %collective-permute-start.3 = (bf16[384,128]{1,0:T(8,128)(2,1)S(1)}, bf16[384,128]{1,0:T(8,128)(2,1)S(1)}, u32[]{:S(2)}, u32[]{:S(2)}) collective-permute-start(bf16[384,128]{1,0:T(8,128)(2,1)S(1)} %shard_map.138), channel_id=1, source_target_pairs={{0,2},{1,7},{2,4},{3,1},{4,6},{5,3},{6,0},{7,5},{8,10},{9,15},{10,... | collective-permute-start | bytes 294920 | tf_op jit(solution)/shard_map/ppermute | solution.py:481
  115.5 0.1 dynamic_slice.11
  115.6 0.8 collective-permute-done.1.refs_1_
  116.4 4.9 %collective-permute-done.3.refs_2_ = bf16[384,128]{1,0:T(8,128)(2,1)S(1)} collective-permute-done((bf16[384,128]{1,0:T(8,128)(2,1)S(1)}, bf16[384,128]{1,0:T(8,128)(2,1)S(1)}, u32[]{:S(2)}, u32[]{:S(2)}) %collective-permute-start.3) | collective-permute-done | bytes 98336 | tf_op jit(solution)/shard_map/ppermute | solution.py:481
  121.3 0.0 copy-done
  121.3 0.8 shard_map.139
  122.1 0.0 all-to-all-done.5.f_ref
  122.1 0.7 shard_map.142
  (4 shorter events, 0.1 us)
Async XLA Ops:
  0.6 29.9 %copy-start.1 = (bf16[128,128]{1,0:T(8,128)(2,1)S(1)}, bf16[128,128]{1,0:T(8,128)(2,1)}, u32[]{:S(2)}) copy-start(bf16[128,128]{1,0:T(8,128)(2,1)} %q_ref.1) | copy-start | bytes 98308
  31.6 5.5 %copy-start.4 = (s32[128]{0:T(128)S(1)}, s32[128]{0:T(128)}, u32[]{:S(2)}) copy-start(s32[128]{0:T(128)} %param.17) | copy-start | bytes 1540
  31.6 5.8 %copy-start.5 = (s32[128,128]{1,0:T(8,128)S(1)}, s32[128,128]{1,0:T(8,128)}, u32[]{:S(2)}) copy-start(s32[128,128]{1,0:T(8,128)} %param.16) | copy-start | bytes 196612
  31.6 6.4 %copy-start.2 = (bf16[128,3072]{1,0:T(8,128)(2,1)S(1)}, bf16[128,3072]{1,0:T(8,128)(2,1)}, u32[]{:S(2)}) copy-start(bf16[128,3072]{1,0:T(8,128)(2,1)} %param.15) | copy-start | bytes 2359300
  31.6 18.6 %all-to-all-start.1 = ((bf16[8,512,128]{2,1,0:T(8,128)(2,1)}), bf16[8,512,128]{2,1,0:T(8,128)(2,1)S(1)}, u32[]{:S(2)}, u32[]{:S(2)}) async-start(bf16[8,512,128]{2,1,0:T(8,128)(2,1)} %shard_map.129), calls=%async_computation.1 | async-start | bytes 2097152 | tf_op jit(solution)/shard_map/all_to_all | solution.py:71
  37.1 1.3 %copy-start.3 = (f32[3072]{0:T(1024)S(1)}, f32[3072]{0:T(1024)}, u32[]{:S(2)}) copy-start(f32[3072]{0:T(1024)} %param.13) | copy-start | bytes 36868
  51.7 10.6 %all-to-all-start.2 = ((bf16[8,128,128]{2,1,0:T(8,128)(2,1)}), bf16[8,128,128]{2,1,0:T(8,128)(2,1)S(1)}, u32[]{:S(2)}, u32[]{:S(2)}) async-start(bf16[8,128,128]{2,1,0:T(8,128)(2,1)} %shard_map.131), calls=%async_computation.2 | async-start | bytes 524288 | tf_op jit(solution)/shard_map/all_to_all | solution.py:71
  64.2 11.8 %all-to-all-start.3 = ((bf16[8,224,128]{2,1,0:T(8,128)(2,1)}), bf16[8,224,128]{2,1,0:T(8,128)(2,1)S(1)}, u32[]{:S(2)}, u32[]{:S(2)}) async-start(bf16[8,224,128]{2,1,0:T(8,128)(2,1)} %get-tuple-element.39), calls=%async_computation.3 | async-start | bytes 917504 | tf_op jit(solution)/shard_map/all_to_all | solution.py:71
  78.5 15.1 %all-to-all-start.4 = ((bf16[8,512,128]{2,1,0:T(8,128)(2,1)}), bf16[8,512,128]{2,1,0:T(8,128)(2,1)S(1)}, u32[]{:S(2)}, u32[]{:S(2)}) async-start(bf16[8,512,128]{2,1,0:T(8,128)(2,1)} %shard_map.135), calls=%async_computation.4 | async-start | bytes 2097152 | tf_op jit(solution)/shard_map/all_to_all | solution.py:71
  83.1 7.7 %collective-permute-start = (bf16[4,384,128]{2,1,0:T(8,128)(2,1)S(1)}, bf16[4,384,128]{2,1,0:T(8,128)(2,1)S(1)}, u32[]{:S(2)}, u32[]{:S(2)}) collective-permute-start(bf16[4,384,128]{2,1,0:T(8,128)(2,1)S(1)} %get-tuple-element.48), channel_id=1, source_target_pairs={{0,1},{1,0},{2,3},{3,2},{4,5},{5,4},{6,7},{7,6},{8,9},{9,8},{10,11... | collective-permute-start | bytes 1179656 | tf_op jit(solution)/shard_map/ppermute | solution.py:451
  95.0 26.4 %copy-start = (bf16[128,384]{1,0:T(8,128)(2,1)S(1)}, bf16[128,384]{1,0:T(8,128)(2,1)}, u32[]{:S(2)}) copy-start(bf16[128,384]{1,0:T(8,128)(2,1)} %residual_ref.1) | copy-start | bytes 294916
  95.0 27.1 %all-to-all-start.5 = ((bf16[8,304,128]{2,1,0:T(8,128)(2,1)}), bf16[8,304,128]{2,1,0:T(8,128)(2,1)S(1)}, u32[]{:S(2)}, u32[]{:S(2)}) async-start(bf16[8,304,128]{2,1,0:T(8,128)(2,1)} %get-tuple-element.59), calls=%async_computation.5 | async-start | bytes 1245184 | tf_op jit(solution)/shard_map/all_to_all | solution.py:71
  101.7 9.9 %collective-permute-start.2 = (bf16[384,128]{1,0:T(8,128)(2,1)S(1)}, bf16[384,128]{1,0:T(8,128)(2,1)S(1)}, u32[]{:S(2)}, u32[]{:S(2)}) collective-permute-start(bf16[384,128]{1,0:T(8,128)(2,1)S(1)} %get-tuple-element.56), channel_id=1, source_target_pairs={{0,2},{1,7},{2,4},{3,1},{4,6},{5,3},{6,0},{7,5},{8,10},{9,15},{10,... | collective-permute-start | bytes 294920 | tf_op jit(solution)/shard_map/ppermute | solution.py:481
  106.2 10.2 %collective-permute-start.1 = (bf16[384,128]{1,0:T(8,128)(2,1)S(1)}, bf16[384,128]{1,0:T(8,128)(2,1)S(1)}, u32[]{:S(2)}, u32[]{:S(2)}) collective-permute-start(bf16[384,128]{1,0:T(8,128)(2,1)S(1)} %get-tuple-element.54), channel_id=1, source_target_pairs={{0,6},{1,3},{2,0},{3,5},{4,2},{5,7},{6,4},{7,1},{8,14},{9,11},{10,... | collective-permute-start | bytes 294920 | tf_op jit(solution)/shard_map/ppermute | solution.py:481
  111.7 9.7 %collective-permute-start.3 = (bf16[384,128]{1,0:T(8,128)(2,1)S(1)}, bf16[384,128]{1,0:T(8,128)(2,1)S(1)}, u32[]{:S(2)}, u32[]{:S(2)}) collective-permute-start(bf16[384,128]{1,0:T(8,128)(2,1)S(1)} %shard_map.138), channel_id=1, source_target_pairs={{0,2},{1,7},{2,4},{3,1},{4,6},{5,3},{6,0},{7,5},{8,10},{9,15},{10,... | collective-permute-start | bytes 294920 | tf_op jit(solution)/shard_map/ppermute | solution.py:481

commit v4 on v3

--- a/solution.py
+++ b/solution.py
@@ -79,11 +79,11 @@
         copy.wait()
 
 
-def first_payload(k_ref, v_ref, w_ref, o_ref, block_ref, sems):
-    block_ref[0:TOK] = k_ref[...]
-    block_ref[TOK : 2 * TOK] = v_ref[...]
-    block_ref[2 * TOK : 2 * TOK + SHARD] = w_ref[...]
-    repeat(block_ref, o_ref, sems)
+def first_payload(k_ref, v_ref, w_ref, o_ref):
+    for i in range(SIDE):
+        o_ref[i, 0:TOK] = k_ref[...]
+        o_ref[i, TOK : 2 * TOK] = v_ref[...]
+        o_ref[i, 2 * TOK : 2 * TOK + SHARD] = w_ref[...]
 
 
 def second_payload(g_ref, q_ref, o_ref, block_ref, sems):
@@ -343,11 +343,9 @@
     row_spec = whole((SIDE, STRIP + TOK, FEAT))
     sent = call(
         first_payload,
-        far((SIDE, 2 * TOK + SHARD, FEAT)),
+        out((SIDE, 2 * TOK + SHARD, FEAT)),
         [own, own, whole((SHARD, FEAT))],
         data=1 << 20,
-        out_specs=anywhere,
-        scratch_shapes=scratch(2 * TOK + SHARD),
     )(*hbm(keys, values, w_out.T))
     kvw = swap(sent, COL)
 
@@ -399,7 +397,7 @@
     half_spec = whole((FEAT, BLOCK))
     part, mean_key, part_lse = call(
         forward,
-        (far((FEAT, BLOCK)), far((FEAT, BLOCK)), out((STATS, TOK), F32)),
+        (out((FEAT, BLOCK)), out((FEAT, BLOCK)), out((STATS, TOK), F32)),
         [query_spec, key_spec, value_spec, bias_spec],
         flops=24 * HD * pair_count,
         data=2 << 20,
@@ -410,7 +408,7 @@
         (far((SIDE, FEAT + 6 * STATS, TOK)), out((STATS, TOK), F32)),
         [half_spec, stat_spec, whole((SIDE, FEAT, TOK))],
         data=2 << 20,
-    )(*hbm(part), part_lse, grad_t)
+    )(part, part_lse, grad_t)
     parts = swap(sent, ROW)
     block_specs = [
         query_spec,
@@ -423,7 +421,7 @@
     ]
     query_share = call(
         query_grad,
-        far((FEAT, BLOCK)),
+        out((FEAT, BLOCK)),
         block_specs,
         flops=24 * HD * pair_count,
         data=3 << 20,
@@ -467,7 +465,7 @@
             pltpu.VMEM((SIDE, STRIP + TOK, FEAT), BF),
             pltpu.SemaphoreType.DMA((SIDE,)),
         ],
-    )(*hbm(query_share, mean_key), part_lse, part_delta, lse, delta, attended, gated_t)
+    )(query_share, mean_key, part_lse, part_delta, lse, delta, attended, gated_t)
     got_row = swap(sent_row, ROW)
     got_row, chunks = lax.optimization_barrier((got_row, chunks))
     mine, far_chunk, ahead_chunk, behind_chunk = chunks

time: 124 us -> 121 us (0.976)
  the two profiles are of different devices: /device:TPU:64 before, /device:TPU:32 now
where the time goes in v4:
time: 121 us; the launch traced here: 120 us
  waiting for transfers between devices  32.4 us (27%)
  starting transfers between devices  30.7 us (25%)
  blocking collectives  29.7 us (25%)
  Pallas kernels  22.4 us (19%)
  local copies, waits for them, and re-layouts  3 us (2%)
    all_to_all x1, blocking collectives, swap(): return lax.all_to_all(a, axes, 0, 0, tiled=True)  29.7 us
    all_to_all x5, waiting for transfers between devices, swap(): return lax.all_to_all(a, axes, 0, 0, tiled=True)  23.2 us
    all_to_all x5, starting transfers between devices, swap(): return lax.all_to_all(a, axes, 0, 0, tiled=True)  18.7 us
    ppermute x3, starting transfers between devices, pass_on(): return lax.ppermute(a, FSDP, pairs)  9.87 us
    ppermute x3, waiting for transfers between devices, pass_on(): return lax.ppermute(a, FSDP, pairs)  9.19 us
    pallas_call x1, Pallas kernels, local(): call(key_grads, far(col_shape), block_specs, flops=32 * HD * pair_count,...  5.53 us
    pallas_call x1, Pallas kernels, local(): call(forward, (out((FEAT, BLOCK)), out((FEAT, BLOCK)), out((STATS, TOK),...  3.49 us
    pallas_call x1, Pallas kernels, local(): call(query_grad, out((FEAT, BLOCK)), block_specs, flops=24 * HD * pair_co...  3.26 us
  transfers between devices with their start and end apart: 9, of which 6 were waited for; matrix products, arithmetic and copies ran while one was open for 2% of the time, Pallas kernels for 12%

profile of v4, /device:TPU:32, one launch (start us, length us, event | category | flops | bytes accessed | tf_op | source)
XLA Modules:
  0.0 119.9 jit_solution(13316497115945432203)
XLA Ops:
  0.6 0.0 copy-start.3
  0.6 0.9 shard_map.128
  1.5 29.7 %all_to_all.30.g_ref.k_ref.v_ref = bf16[8,304,128]{2,1,0:T(8,128)(2,1)S(1)} all-to-all(bf16[8,304,128]{2,1,0:T(8,128)(2,1)S(1)} %shard_map.128), channel_id=1, replica_groups=mesh['z'=8,'x'=4,'yl'=2,'yh'=4,'core'=2] {'z'}, dimensions={0} | all-to-all | bytes 1245184 | tf_op jit(solution)/shard_map/all_to_all | solution.py:71
  31.2 0.0 copy-done.3
  31.2 1.1 shard_map.129
  32.3 0.0 copy-start.6
  32.3 0.0 copy-start.7
  32.3 0.0 copy-start.4
  32.4 4.6 %all-to-all-start.1 = ((bf16[8,512,128]{2,1,0:T(8,128)(2,1)}), bf16[8,512,128]{2,1,0:T(8,128)(2,1)S(1)}, u32[]{:S(2)}, u32[]{:S(2)}) async-start(bf16[8,512,128]{2,1,0:T(8,128)(2,1)} %shard_map.129), calls=%async_computation.1 | async-start | bytes 2097152 | tf_op jit(solution)/shard_map/all_to_all | solution.py:71
  36.9 0.0 copy-start.5
  36.9 0.0 copy-done.6
  36.9 0.1 reshape.33
  37.1 0.1 eq.36
  37.2 0.1 eq.42
  37.3 0.0 copy-done.7
  37.3 0.3 fusion.3
  37.6 0.1 broadcast_in_dim.23
  37.7 0.1 reshape.34.bias_ref
  37.8 0.0 copy-done.4
  37.8 0.4 copy.17
  38.2 0.0 copy-done.5
  38.2 0.5 multiply_convert_fusion
  38.7 0.1 copy.18
  38.8 12.6 %all-to-all-done.1.q_ref.w_ref = bf16[8,512,128]{2,1,0:T(8,128)(2,1)S(1)} async-done(((bf16[8,512,128]{2,1,0:T(8,128)(2,1)}), bf16[8,512,128]{2,1,0:T(8,128)(2,1)S(1)}, u32[]{:S(2)}, u32[]{:S(2)}) %all-to-all-start.1) | async-done | bytes 1048608 | tf_op jit(solution)/shard_map/all_to_all | solution.py:71
  51.3 0.3 copy.19.gated_ref
  51.6 1.3 %shard_map.131 = bf16[8,128,128]{2,1,0:T(8,128)(2,1)} custom-call(bf16[128,3072]{1,0:T(8,128)(2,1)S(1)} %copy.19.gated_ref, bf16[8,512,128]{2,1,0:T(8,128)(2,1)S(1)} %all-to-all-done.1.q_ref.w_ref), custom_call_target="tpu_custom_call" | custom-call | flops 100663296 | bytes 2097152 | tf_op jit(solution)/shard_map/pallas_call | solution.py:380
  52.9 3.4 %all-to-all-start.2 = ((bf16[8,128,128]{2,1,0:T(8,128)(2,1)}), bf16[8,128,128]{2,1,0:T(8,128)(2,1)S(1)}, u32[]{:S(2)}, u32[]{:S(2)}) async-start(bf16[8,128,128]{2,1,0:T(8,128)(2,1)} %shard_map.131), calls=%async_computation.2 | async-start | bytes 524288 | tf_op jit(solution)/shard_map/all_to_all | solution.py:71
  56.3 3.5 %shard_map.130 = (bf16[128,1024]{1,0:T(8,128)(2,1)S(1)}, bf16[128,1024]{1,0:T(8,128)(2,1)S(1)}, f32[16,128]{1,0:T(8,128)S(1)}) custom-call(bf16[8,512,128]{2,1,0:T(8,128)(2,1)S(1)} %all-to-all-done.1.q_ref.w_ref, bf16[8,304,128]{2,1,0:T(8,128)(2,1)S(1)} %all_to_all.30.g_ref.k_ref.v_ref, bf16[8,304,128]{2,1,0:T(8,128)(2,1)S(1)} %all_to_all.30.g_ref.k_ref.v_ref, ...), custom_call_target="tpu_custom_call" | custom-call | flops 3221225472 | bytes 2097152 | tf_op jit(solution)/shard_map/pallas_call | solution.py:398
  59.8 3.7 %all-to-all-done.2.grad_ref = bf16[8,128,128]{2,1,0:T(8,128)(2,1)S(1)} async-done(((bf16[8,128,128]{2,1,0:T(8,128)(2,1)}), bf16[8,128,128]{2,1,0:T(8,128)(2,1)S(1)}, u32[]{:S(2)}, u32[]{:S(2)}) %all-to-all-start.2) | async-done | bytes 262176 | tf_op jit(solution)/shard_map/all_to_all | solution.py:71
  63.5 0.9 shard_map.132
  64.5 3.5 %all-to-all-start.3 = ((bf16[8,224,128]{2,1,0:T(8,128)(2,1)}), bf16[8,224,128]{2,1,0:T(8,128)(2,1)S(1)}, u32[]{:S(2)}, u32[]{:S(2)}) async-start(bf16[8,224,128]{2,1,0:T(8,128)(2,1)} %get-tuple-element.39), calls=%async_computation.3 | async-start | bytes 917504 | tf_op jit(solution)/shard_map/all_to_all | solution.py:71
  67.9 3.3 %shard_map.133.grad_ref = bf16[128,1024]{1,0:T(8,128)(2,1)S(1)} custom-call(bf16[8,512,128]{2,1,0:T(8,128)(2,1)S(1)} %all-to-all-done.1.q_ref.w_ref, bf16[8,304,128]{2,1,0:T(8,128)(2,1)S(1)} %all_to_all.30.g_ref.k_ref.v_ref, bf16[8,304,128]{2,1,0:T(8,128)(2,1)S(1)} %all_to_all.30.g_ref.k_ref.v_ref, bf16[8,128,128]{2,1,0:T(8,128)(2,1)S(1)} %all-to-all-done.2.grad_ref, ...), custom_call_target="tpu_custom_call" | custom-call | flops 3221225472 | bytes 3145728 | tf_op jit(solution)/shard_map/pallas_call | solution.py:422
  71.2 0.0 copy-start
  71.2 0.7 copy-done
  71.9 4.3 %all-to-all-done.3.d_ref = bf16[8,224,128]{2,1,0:T(8,128)(2,1)S(1)} async-done(((bf16[8,224,128]{2,1,0:T(8,128)(2,1)}), bf16[8,224,128]{2,1,0:T(8,128)(2,1)S(1)}, u32[]{:S(2)}, u32[]{:S(2)}) %all-to-all-start.3) | async-done | bytes 458784 | tf_op jit(solution)/shard_map/all_to_all | solution.py:71
  76.2 0.2 shard_map.134
  76.4 0.0 copy-start.1
  76.4 0.9 copy-done.1
  77.3 1.3 %shard_map.135 = bf16[8,512,128]{2,1,0:T(8,128)(2,1)} custom-call(bf16[128,1024]{1,0:T(8,128)(2,1)S(1)} %copy-done.1, bf16[128,1024]{1,0:T(8,128)(2,1)S(1)} %get-tuple-element.42.mean_ref, f32[16,128]{1,0:T(8,128)S(1)} %get-tuple-element.37.lse_ref, f32[16,128]{1,0:T(8,128)S(1)} %get-tuple-element.40.delta_ref, ...), custom_call_target="tpu_custom_call" | custom-call | flops 100663296 | bytes 3145728 | tf_op jit(solution)/shard_map/pallas_call | solution.py:457
  78.6 3.6 %all-to-all-start.4 = ((bf16[8,512,128]{2,1,0:T(8,128)(2,1)}), bf16[8,512,128]{2,1,0:T(8,128)(2,1)S(1)}, u32[]{:S(2)}, u32[]{:S(2)}) async-start(bf16[8,512,128]{2,1,0:T(8,128)(2,1)} %shard_map.135), calls=%async_computation.4 | async-start | bytes 2097152 | tf_op jit(solution)/shard_map/all_to_all | solution.py:71
  82.2 0.1 pad_add_fusion.place_ref
  82.3 1.0 shard_map.136
  83.3 2.1 %collective-permute-start = (bf16[4,384,128]{2,1,0:T(8,128)(2,1)S(1)}, bf16[4,384,128]{2,1,0:T(8,128)(2,1)S(1)}, u32[]{:S(2)}, u32[]{:S(2)}) collective-permute-start(bf16[4,384,128]{2,1,0:T(8,128)(2,1)S(1)} %get-tuple-element.48), channel_id=1, source_target_pairs={{0,1},{1,0},{2,3},{3,2},{4,5},{5,4},{6,7},{7,6},{8,9},{9,8},{10,11... | collective-permute-start | bytes 1179656 | tf_op jit(solution)/shard_map/ppermute | solution.py:449
  85.4 5.5 %shard_map.140.f_in = bf16[8,304,128]{2,1,0:T(8,128)(2,1)} custom-call(bf16[8,512,128]{2,1,0:T(8,128)(2,1)S(1)} %all-to-all-done.1.q_ref.w_ref, bf16[8,304,128]{2,1,0:T(8,128)(2,1)S(1)} %all_to_all.30.g_ref.k_ref.v_ref, bf16[8,304,128]{2,1,0:T(8,128)(2,1)S(1)} %all_to_all.30.g_ref.k_ref.v_ref, bf16[8,128,128]{2,1,0:T(8,128)(2,1)S(1)} %all-to-all-done.2.grad_ref, ...), custom_call_target="tpu_custom_call" | custom-call | flops 4294967296 | bytes 3145728 | tf_op jit(solution)/shard_map/pallas_call | solution.py:488
  90.9 0.0 collective-permute-done.got_ref
  90.9 0.6 shard_map.137
  91.6 2.5 %all-to-all-done.4.e_ref = bf16[8,512,128]{2,1,0:T(8,128)(2,1)S(1)} async-done(((bf16[8,512,128]{2,1,0:T(8,128)(2,1)}), bf16[8,512,128]{2,1,0:T(8,128)(2,1)S(1)}, u32[]{:S(2)}, u32[]{:S(2)}) %all-to-all-start.4) | async-done | bytes 1048608 | tf_op jit(solution)/shard_map/all_to_all | solution.py:71
  94.1 1.4 %shard_map.141 = (bf16[128,128]{1,0:T(8,128)(2,1)}, bf16[8,304,128]{2,1,0:T(8,128)(2,1)}) custom-call(bf16[8,512,128]{2,1,0:T(8,128)(2,1)S(1)} %all-to-all-done.4.e_ref, bf16[8,304,128]{2,1,0:T(8,128)(2,1)} %shard_map.140.f_in), custom_call_target="tpu_custom_call", output_to_operand_aliasing={{1}: (1, {})} | custom-call | flops 1 | bytes 2097152 | tf_op jit(solution)/shard_map/pallas_call | solution.py:497
  95.5 0.0 copy-start.2
  95.5 3.7 %all-to-all-start.5 = ((bf16[8,304,128]{2,1,0:T(8,128)(2,1)}), bf16[8,304,128]{2,1,0:T(8,128)(2,1)S(1)}, u32[]{:S(2)}, u32[]{:S(2)}) async-start(bf16[8,304,128]{2,1,0:T(8,128)(2,1)} %get-tuple-element.59), calls=%async_computation.5 | async-start | bytes 1245184 | tf_op jit(solution)/shard_map/all_to_all | solution.py:71
  99.2 2.7 %collective-permute-start.2 = (bf16[384,128]{1,0:T(8,128)(2,1)S(1)}, bf16[384,128]{1,0:T(8,128)(2,1)S(1)}, u32[]{:S(2)}, u32[]{:S(2)}) collective-permute-start(bf16[384,128]{1,0:T(8,128)(2,1)S(1)} %get-tuple-element.56), channel_id=1, source_target_pairs={{0,2},{1,7},{2,4},{3,1},{4,6},{5,3},{6,0},{7,5},{8,10},{9,15},{10,... | collective-permute-start | bytes 294920 | tf_op jit(solution)/shard_map/ppermute | solution.py:479
  101.9 5.3 %collective-permute-start.1 = (bf16[384,128]{1,0:T(8,128)(2,1)S(1)}, bf16[384,128]{1,0:T(8,128)(2,1)S(1)}, u32[]{:S(2)}, u32[]{:S(2)}) collective-permute-start(bf16[384,128]{1,0:T(8,128)(2,1)S(1)} %get-tuple-element.54), channel_id=1, source_target_pairs={{0,6},{1,3},{2,0},{3,5},{4,2},{5,7},{6,4},{7,1},{8,14},{9,11},{10,... | collective-permute-start | bytes 294920 | tf_op jit(solution)/shard_map/ppermute | solution.py:479
  107.2 2.6 %collective-permute-done.2.got_ref = bf16[384,128]{1,0:T(8,128)(2,1)S(1)} collective-permute-done((bf16[384,128]{1,0:T(8,128)(2,1)S(1)}, bf16[384,128]{1,0:T(8,128)(2,1)S(1)}, u32[]{:S(2)}, u32[]{:S(2)}) %collective-permute-start.2) | collective-permute-done | bytes 98336 | tf_op jit(solution)/shard_map/ppermute | solution.py:479
  109.8 1.9 %collective-permute-start.3 = (bf16[384,128]{1,0:T(8,128)(2,1)S(1)}, bf16[384,128]{1,0:T(8,128)(2,1)S(1)}, u32[]{:S(2)}, u32[]{:S(2)}) collective-permute-start(bf16[384,128]{1,0:T(8,128)(2,1)S(1)} %shard_map.138), channel_id=1, source_target_pairs={{0,2},{1,7},{2,4},{3,1},{4,6},{5,3},{6,0},{7,5},{8,10},{9,15},{10,... | collective-permute-start | bytes 294920 | tf_op jit(solution)/shard_map/ppermute | solution.py:479
  111.8 0.1 dynamic_slice.11
  111.8 0.0 collective-permute-done.1.refs_1_
  111.9 6.6 %collective-permute-done.3.refs_2_ = bf16[384,128]{1,0:T(8,128)(2,1)S(1)} collective-permute-done((bf16[384,128]{1,0:T(8,128)(2,1)S(1)}, bf16[384,128]{1,0:T(8,128)(2,1)S(1)}, u32[]{:S(2)}, u32[]{:S(2)}) %collective-permute-start.3) | collective-permute-done | bytes 98336 | tf_op jit(solution)/shard_map/ppermute | solution.py:479
  118.4 0.0 copy-done.2
  118.4 0.8 shard_map.139
  119.2 0.0 all-to-all-done.5.f_ref
  119.2 0.7 shard_map.142
  (4 shorter events, 0.1 us)
Async XLA Ops:
  0.6 30.6 %copy-start.3 = (bf16[128,128]{1,0:T(8,128)(2,1)S(1)}, bf16[128,128]{1,0:T(8,128)(2,1)}, u32[]{:S(2)}) copy-start(bf16[128,128]{1,0:T(8,128)(2,1)} %q_ref.1) | copy-start | bytes 98308
  32.3 4.6 %copy-start.6 = (s32[128]{0:T(128)S(1)}, s32[128]{0:T(128)}, u32[]{:S(2)}) copy-start(s32[128]{0:T(128)} %param.17) | copy-start | bytes 1540
  32.3 4.9 %copy-start.7 = (s32[128,128]{1,0:T(8,128)S(1)}, s32[128,128]{1,0:T(8,128)}, u32[]{:S(2)}) copy-start(s32[128,128]{1,0:T(8,128)} %param.16) | copy-start | bytes 196612
  32.3 5.5 %copy-start.4 = (bf16[128,3072]{1,0:T(8,128)(2,1)S(1)}, bf16[128,3072]{1,0:T(8,128)(2,1)}, u32[]{:S(2)}) copy-start(bf16[128,3072]{1,0:T(8,128)(2,1)} %param.15) | copy-start | bytes 2359300
  32.4 19.0 %all-to-all-start.1 = ((bf16[8,512,128]{2,1,0:T(8,128)(2,1)}), bf16[8,512,128]{2,1,0:T(8,128)(2,1)S(1)}, u32[]{:S(2)}, u32[]{:S(2)}) async-start(bf16[8,512,128]{2,1,0:T(8,128)(2,1)} %shard_map.129), calls=%async_computation.1 | async-start | bytes 2097152 | tf_op jit(solution)/shard_map/all_to_all | solution.py:71
  36.9 1.3 %copy-start.5 = (f32[3072]{0:T(1024)S(1)}, f32[3072]{0:T(1024)}, u32[]{:S(2)}) copy-start(f32[3072]{0:T(1024)} %param.13) | copy-start | bytes 36868
  52.9 10.6 %all-to-all-start.2 = ((bf16[8,128,128]{2,1,0:T(8,128)(2,1)}), bf16[8,128,128]{2,1,0:T(8,128)(2,1)S(1)}, u32[]{:S(2)}, u32[]{:S(2)}) async-start(bf16[8,128,128]{2,1,0:T(8,128)(2,1)} %shard_map.131), calls=%async_computation.2 | async-start | bytes 524288 | tf_op jit(solution)/shard_map/all_to_all | solution.py:71
  64.5 11.8 %all-to-all-start.3 = ((bf16[8,224,128]{2,1,0:T(8,128)(2,1)}), bf16[8,224,128]{2,1,0:T(8,128)(2,1)S(1)}, u32[]{:S(2)}, u32[]{:S(2)}) async-start(bf16[8,224,128]{2,1,0:T(8,128)(2,1)} %get-tuple-element.39), calls=%async_computation.3 | async-start | bytes 917504 | tf_op jit(solution)/shard_map/all_to_all | solution.py:71
  71.2 0.7 copy-start
  76.4 1.0 copy-start.1
  78.6 15.5 %all-to-all-start.4 = ((bf16[8,512,128]{2,1,0:T(8,128)(2,1)}), bf16[8,512,128]{2,1,0:T(8,128)(2,1)S(1)}, u32[]{:S(2)}, u32[]{:S(2)}) async-start(bf16[8,512,128]{2,1,0:T(8,128)(2,1)} %shard_map.135), calls=%async_computation.4 | async-start | bytes 2097152 | tf_op jit(solution)/shard_map/all_to_all | solution.py:71
  83.3 7.6 %collective-permute-start = (bf16[4,384,128]{2,1,0:T(8,128)(2,1)S(1)}, bf16[4,384,128]{2,1,0:T(8,128)(2,1)S(1)}, u32[]{:S(2)}, u32[]{:S(2)}) collective-permute-start(bf16[4,384,128]{2,1,0:T(8,128)(2,1)S(1)} %get-tuple-element.48), channel_id=1, source_target_pairs={{0,1},{1,0},{2,3},{3,2},{4,5},{5,4},{6,7},{7,6},{8,9},{9,8},{10,11... | collective-permute-start | bytes 1179656 | tf_op jit(solution)/shard_map/ppermute | solution.py:449
  95.5 22.9 %copy-start.2 = (bf16[128,384]{1,0:T(8,128)(2,1)S(1)}, bf16[128,384]{1,0:T(8,128)(2,1)}, u32[]{:S(2)}) copy-start(bf16[128,384]{1,0:T(8,128)(2,1)} %residual_ref.1) | copy-start | bytes 294916
  95.5 23.7 %all-to-all-start.5 = ((bf16[8,304,128]{2,1,0:T(8,128)(2,1)}), bf16[8,304,128]{2,1,0:T(8,128)(2,1)S(1)}, u32[]{:S(2)}, u32[]{:S(2)}) async-start(bf16[8,304,128]{2,1,0:T(8,128)(2,1)} %get-tuple-element.59), calls=%async_computation.5 | async-start | bytes 1245184 | tf_op jit(solution)/shard_map/all_to_all | solution.py:71
  99.2 10.6 %collective-permute-start.2 = (bf16[384,128]{1,0:T(8,128)(2,1)S(1)}, bf16[384,128]{1,0:T(8,128)(2,1)S(1)}, u32[]{:S(2)}, u32[]{:S(2)}) collective-permute-start(bf16[384,128]{1,0:T(8,128)(2,1)S(1)} %get-tuple-element.56), channel_id=1, source_target_pairs={{0,2},{1,7},{2,4},{3,1},{4,6},{5,3},{6,0},{7,5},{8,10},{9,15},{10,... | collective-permute-start | bytes 294920 | tf_op jit(solution)/shard_map/ppermute | solution.py:479
  101.9 9.9 %collective-permute-start.1 = (bf16[384,128]{1,0:T(8,128)(2,1)S(1)}, bf16[384,128]{1,0:T(8,128)(2,1)S(1)}, u32[]{:S(2)}, u32[]{:S(2)}) collective-permute-start(bf16[384,128]{1,0:T(8,128)(2,1)S(1)} %get-tuple-element.54), channel_id=1, source_target_pairs={{0,6},{1,3},{2,0},{3,5},{4,2},{5,7},{6,4},{7,1},{8,14},{9,11},{10,... | collective-permute-start | bytes 294920 | tf_op jit(solution)/shard_map/ppermute | solution.py:479
  109.8 8.6 %collective-permute-start.3 = (bf16[384,128]{1,0:T(8,128)(2,1)S(1)}, bf16[384,128]{1,0:T(8,128)(2,1)S(1)}, u32[]{:S(2)}, u32[]{:S(2)}) collective-permute-start(bf16[384,128]{1,0:T(8,128)(2,1)S(1)} %shard_map.138), channel_id=1, source_target_pairs={{0,2},{1,7},{2,4},{3,1},{4,6},{5,3},{6,0},{7,5},{8,10},{9,15},{10,... | collective-permute-start | bytes 294920 | tf_op jit(solution)/shard_map/ppermute | solution.py:479

commit v5 on v4

--- a/solution.py
+++ b/solution.py
@@ -219,7 +219,7 @@
     att_ref[...] = jnp.concatenate(heads, axis=0).T.astype(BF)
 
 
-def branch_rows(place_ref, att_ref, w_ref, keep_ref, send_ref, all_ref):
+def branch_rows(core_ref, att_ref, w_ref, keep_ref, send_ref, all_ref):
     att = att_ref[...]
     for i in range(SIDE):
         part = lax.dot_general(
@@ -227,14 +227,14 @@
         ).astype(BF)
         for j in range(SIDE):
             all_ref[j, i * SHARD : (i + 1) * SHARD] = part[j * SHARD : (j + 1) * SHARD]
-    core = place_ref[1]
+    core = core_ref[0]
     for i in range(PAIRS):
         keep_ref[i] = all_ref[2 * i + core]
         send_ref[i] = all_ref[2 * i + 1 - core]
 
 
-def add_halves(place_ref, keep_ref, got_ref, own_ref, far_ref, ahead_ref, behind_ref):
-    pair, ahead = place_ref[0], 1 - 2 * place_ref[1]
+def add_halves(pair_ref, core_ref, keep_ref, got_ref, own_ref, far_ref, ahead_ref, behind_ref):
+    pair, ahead = pair_ref[0], 1 - 2 * core_ref[0]
     steps = ((own_ref, 0), (far_ref, 2), (ahead_ref, ahead), (behind_ref, -ahead))
     for ref, step in steps:
         i = lax.rem(pair + step + PAIRS, PAIRS)
@@ -437,7 +437,8 @@
         scratch_shapes=[pltpu.VMEM((SIDE, STATS, TOK), F32)],
     )(p.reshape(1).astype(jnp.int32), parts)
     scalar = pl.BlockSpec(memory_space=pltpu.SMEM)
-    place = jnp.stack([lax.axis_index("yh"), lax.axis_index("core")]).astype(jnp.int32)
+    core = lax.axis_index("core").reshape(1).astype(jnp.int32)
+    pair = lax.axis_index("yh").reshape(1).astype(jnp.int32)
     keep, send = call(
         branch_rows,
         (out((PAIRS, STRIP, TOK)), out((PAIRS, STRIP, TOK))),
@@ -445,14 +446,14 @@
         flops=2 * TOK * FEAT * SIDE * STRIP,
         data=2 << 20,
         scratch_shapes=[pltpu.VMEM((SIDE, STRIP, TOK), BF)],
-    )(place, attended, wq)
+    )(core, attended, wq)
     got = lax.ppermute(send, "core", [(0, 1), (1, 0)])
     chunks = call(
         add_halves,
         (out((STRIP, TOK)),) * PAIRS,
-        [scalar] + [whole((PAIRS, STRIP, TOK))] * 2,
-        data=2 << 20,
-    )(place, keep, got)
+        [scalar] * 2 + [whole((PAIRS, STRIP, TOK))] * 2,
+        data=2 << 20,
+    )(pair, core, keep, got)
 
     sent_row = call(
         row_payload,

time: 121 us -> 122 us (level)
  the two profiles are of different devices: /device:TPU:32 before, /device:TPU:40 now
where the time goes in v5:
time: 122 us
  starting transfers between devices  35.3 us (29%)
  waiting for transfers between devices  30.7 us (25%)
  blocking collectives  29.7 us (24%)
  Pallas kernels  21.3 us (17%)
  local copies, waits for them, and re-layouts  3 us (2%)
    all_to_all x1, blocking collectives, swap(): return lax.all_to_all(a, axes, 0, 0, tiled=True)  29.7 us
    all_to_all x5, starting transfers between devices, swap(): return lax.all_to_all(a, axes, 0, 0, tiled=True)  23.3 us
    all_to_all x5, waiting for transfers between devices, swap(): return lax.all_to_all(a, axes, 0, 0, tiled=True)  19.5 us
    ppermute x3, waiting for transfers between devices, pass_on(): return lax.ppermute(a, FSDP, pairs)  11.2 us
    ppermute x3, starting transfers between devices, pass_on(): return lax.ppermute(a, FSDP, pairs)  9.86 us
    pallas_call x1, Pallas kernels, local(): call(key_grads, far(col_shape), block_specs, flops=32 * HD * pair_count,...  5.53 us
    pallas_call x1, Pallas kernels, local(): call(forward, (out((FEAT, BLOCK)), out((FEAT, BLOCK)), out((STATS, TOK),...  3.49 us
    pallas_call x1, Pallas kernels, local(): call(query_grad, out((FEAT, BLOCK)), block_specs, flops=24 * HD * pair_co...  3.25 us
  transfers between devices with their start and end apart: 9, of which 6 were waited for; matrix products, arithmetic and copies ran while one was open for 2% of the time, Pallas kernels for 11%

profile of v5, /device:TPU:40, one launch (start us, length us, event | category | flops | bytes accessed | tf_op | source)
XLA Modules:
  0.0 121.7 jit_solution(15021901183242181776)
XLA Ops:
  0.6 0.0 copy-start.3
  0.6 0.9 shard_map.128
  1.5 29.7 %all_to_all.30.g_ref.k_ref.v_ref = bf16[8,304,128]{2,1,0:T(8,128)(2,1)S(1)} all-to-all(bf16[8,304,128]{2,1,0:T(8,128)(2,1)S(1)} %shard_map.128), channel_id=1, replica_groups=mesh['z'=8,'x'=4,'yl'=2,'yh'=4,'core'=2] {'z'}, dimensions={0} | all-to-all | bytes 1245184 | tf_op jit(solution)/shard_map/all_to_all | solution.py:71
  31.2 0.0 copy-done.3
  31.2 1.1 shard_map.129
  32.3 0.0 copy-start.6
  32.3 0.0 copy-start.7
  32.3 0.0 copy-start.4
  32.4 5.9 %all-to-all-start.1 = ((bf16[8,512,128]{2,1,0:T(8,128)(2,1)}), bf16[8,512,128]{2,1,0:T(8,128)(2,1)S(1)}, u32[]{:S(2)}, u32[]{:S(2)}) async-start(bf16[8,512,128]{2,1,0:T(8,128)(2,1)} %shard_map.129), calls=%async_computation.1 | async-start | bytes 2097152 | tf_op jit(solution)/shard_map/all_to_all | solution.py:71
  38.3 0.0 copy-start.5
  38.3 0.0 copy-done.6
  38.3 0.1 reshape.39
  38.4 0.1 eq.36
  38.5 0.1 eq.42
  38.6 0.0 copy-done.7
  38.6 0.3 fusion.3
  38.9 0.1 broadcast_in_dim.23
  39.0 0.1 reshape.40.bias_ref
  39.2 0.0 copy-done.4
  39.2 0.4 copy.17
  39.5 0.0 copy-done.5
  39.6 0.5 multiply_convert_fusion
  40.0 0.1 copy.18
  40.1 11.4 %all-to-all-done.1.q_ref.w_ref = bf16[8,512,128]{2,1,0:T(8,128)(2,1)S(1)} async-done(((bf16[8,512,128]{2,1,0:T(8,128)(2,1)}), bf16[8,512,128]{2,1,0:T(8,128)(2,1)S(1)}, u32[]{:S(2)}, u32[]{:S(2)}) %all-to-all-start.1) | async-done | bytes 1048608 | tf_op jit(solution)/shard_map/all_to_all | solution.py:71
  51.5 0.3 copy.19.gated_ref
  51.8 1.3 %shard_map.131 = bf16[8,128,128]{2,1,0:T(8,128)(2,1)} custom-call(bf16[128,3072]{1,0:T(8,128)(2,1)S(1)} %copy.19.gated_ref, bf16[8,512,128]{2,1,0:T(8,128)(2,1)S(1)} %all-to-all-done.1.q_ref.w_ref), custom_call_target="tpu_custom_call" | custom-call | flops 100663296 | bytes 2097152 | tf_op jit(solution)/shard_map/pallas_call | solution.py:380
  53.0 4.5 %all-to-all-start.2 = ((bf16[8,128,128]{2,1,0:T(8,128)(2,1)}), bf16[8,128,128]{2,1,0:T(8,128)(2,1)S(1)}, u32[]{:S(2)}, u32[]{:S(2)}) async-start(bf16[8,128,128]{2,1,0:T(8,128)(2,1)} %shard_map.131), calls=%async_computation.2 | async-start | bytes 524288 | tf_op jit(solution)/shard_map/all_to_all | solution.py:71
  57.6 3.5 %shard_map.130 = (bf16[128,1024]{1,0:T(8,128)(2,1)S(1)}, bf16[128,1024]{1,0:T(8,128)(2,1)S(1)}, f32[16,128]{1,0:T(8,128)S(1)}) custom-call(bf16[8,512,128]{2,1,0:T(8,128)(2,1)S(1)} %all-to-all-done.1.q_ref.w_ref, bf16[8,304,128]{2,1,0:T(8,128)(2,1)S(1)} %all_to_all.30.g_ref.k_ref.v_ref, bf16[8,304,128]{2,1,0:T(8,128)(2,1)S(1)} %all_to_all.30.g_ref.k_ref.v_ref, ...), custom_call_target="tpu_custom_call" | custom-call | flops 3221225472 | bytes 2097152 | tf_op jit(solution)/shard_map/pallas_call | solution.py:398
  61.1 2.6 %all-to-all-done.2.grad_ref = bf16[8,128,128]{2,1,0:T(8,128)(2,1)S(1)} async-done(((bf16[8,128,128]{2,1,0:T(8,128)(2,1)}), bf16[8,128,128]{2,1,0:T(8,128)(2,1)S(1)}, u32[]{:S(2)}, u32[]{:S(2)}) %all-to-all-start.2) | async-done | bytes 262176 | tf_op jit(solution)/shard_map/all_to_all | solution.py:71
  63.7 0.9 shard_map.132
  64.6 4.6 %all-to-all-start.3 = ((bf16[8,224,128]{2,1,0:T(8,128)(2,1)}), bf16[8,224,128]{2,1,0:T(8,128)(2,1)S(1)}, u32[]{:S(2)}, u32[]{:S(2)}) async-start(bf16[8,224,128]{2,1,0:T(8,128)(2,1)} %get-tuple-element.39), calls=%async_computation.3 | async-start | bytes 917504 | tf_op jit(solution)/shard_map/all_to_all | solution.py:71
  69.2 3.3 %shard_map.133.grad_ref = bf16[128,1024]{1,0:T(8,128)(2,1)S(1)} custom-call(bf16[8,512,128]{2,1,0:T(8,128)(2,1)S(1)} %all-to-all-done.1.q_ref.w_ref, bf16[8,304,128]{2,1,0:T(8,128)(2,1)S(1)} %all_to_all.30.g_ref.k_ref.v_ref, bf16[8,304,128]{2,1,0:T(8,128)(2,1)S(1)} %all_to_all.30.g_ref.k_ref.v_ref, bf16[8,128,128]{2,1,0:T(8,128)(2,1)S(1)} %all-to-all-done.2.grad_ref, ...), custom_call_target="tpu_custom_call" | custom-call | flops 3221225472 | bytes 3145728 | tf_op jit(solution)/shard_map/pallas_call | solution.py:422
  72.4 0.0 copy-start
  72.4 0.7 copy-done
  73.1 3.2 %all-to-all-done.3.d_ref = bf16[8,224,128]{2,1,0:T(8,128)(2,1)S(1)} async-done(((bf16[8,224,128]{2,1,0:T(8,128)(2,1)}), bf16[8,224,128]{2,1,0:T(8,128)(2,1)S(1)}, u32[]{:S(2)}, u32[]{:S(2)}) %all-to-all-start.3) | async-done | bytes 458784 | tf_op jit(solution)/shard_map/all_to_all | solution.py:71
  76.4 0.2 shard_map.134
  76.6 0.0 copy-start.1
  76.6 0.9 copy-done.1
  77.5 1.3 %shard_map.135 = bf16[8,512,128]{2,1,0:T(8,128)(2,1)} custom-call(bf16[128,1024]{1,0:T(8,128)(2,1)S(1)} %copy-done.1, bf16[128,1024]{1,0:T(8,128)(2,1)S(1)} %get-tuple-element.42.mean_ref, f32[16,128]{1,0:T(8,128)S(1)} %get-tuple-element.37.lse_ref, f32[16,128]{1,0:T(8,128)S(1)} %get-tuple-element.40.delta_ref, ...), custom_call_target="tpu_custom_call" | custom-call | flops 100663296 | bytes 3145728 | tf_op jit(solution)/shard_map/pallas_call | solution.py:458
  78.8 4.6 %all-to-all-start.4 = ((bf16[8,512,128]{2,1,0:T(8,128)(2,1)}), bf16[8,512,128]{2,1,0:T(8,128)(2,1)S(1)}, u32[]{:S(2)}, u32[]{:S(2)}) async-start(bf16[8,512,128]{2,1,0:T(8,128)(2,1)} %shard_map.135), calls=%async_computation.4 | async-start | bytes 2097152 | tf_op jit(solution)/shard_map/all_to_all | solution.py:71
  83.5 0.4 shard_map.136
  83.9 2.1 %collective-permute-start = (bf16[4,384,128]{2,1,0:T(8,128)(2,1)S(1)}, bf16[4,384,128]{2,1,0:T(8,128)(2,1)S(1)}, u32[]{:S(2)}, u32[]{:S(2)}) collective-permute-start(bf16[4,384,128]{2,1,0:T(8,128)(2,1)S(1)} %get-tuple-element.48), channel_id=1, source_target_pairs={{0,1},{1,0},{2,3},{3,2},{4,5},{5,4},{6,7},{7,6},{8,9},{9,8},{10,11... | collective-permute-start | bytes 1179656 | tf_op jit(solution)/shard_map/ppermute | solution.py:450
  86.0 5.5 %shard_map.140.f_in = bf16[8,304,128]{2,1,0:T(8,128)(2,1)} custom-call(bf16[8,512,128]{2,1,0:T(8,128)(2,1)S(1)} %all-to-all-done.1.q_ref.w_ref, bf16[8,304,128]{2,1,0:T(8,128)(2,1)S(1)} %all_to_all.30.g_ref.k_ref.v_ref, bf16[8,304,128]{2,1,0:T(8,128)(2,1)S(1)} %all_to_all.30.g_ref.k_ref.v_ref, bf16[8,128,128]{2,1,0:T(8,128)(2,1)S(1)} %all-to-all-done.2.grad_ref, ...), custom_call_target="tpu_custom_call" | custom-call | flops 4294967296 | bytes 3145728 | tf_op jit(solution)/shard_map/pallas_call | solution.py:489
  91.5 0.0 collective-permute-done.got_ref
  91.5 0.1 shard_map.137
  91.6 2.2 %all-to-all-done.4.e_ref = bf16[8,512,128]{2,1,0:T(8,128)(2,1)S(1)} async-done(((bf16[8,512,128]{2,1,0:T(8,128)(2,1)}), bf16[8,512,128]{2,1,0:T(8,128)(2,1)S(1)}, u32[]{:S(2)}, u32[]{:S(2)}) %all-to-all-start.4) | async-done | bytes 1048608 | tf_op jit(solution)/shard_map/all_to_all | solution.py:71
  93.8 1.4 %shard_map.141 = (bf16[128,128]{1,0:T(8,128)(2,1)}, bf16[8,304,128]{2,1,0:T(8,128)(2,1)}) custom-call(bf16[8,512,128]{2,1,0:T(8,128)(2,1)S(1)} %all-to-all-done.4.e_ref, bf16[8,304,128]{2,1,0:T(8,128)(2,1)} %shard_map.140.f_in), custom_call_target="tpu_custom_call", output_to_operand_aliasing={{1}: (1, {})} | custom-call | flops 1 | bytes 2097152 | tf_op jit(solution)/shard_map/pallas_call | solution.py:498
  95.3 0.0 copy-start.2
  95.3 3.7 %all-to-all-start.5 = ((bf16[8,304,128]{2,1,0:T(8,128)(2,1)}), bf16[8,304,128]{2,1,0:T(8,128)(2,1)S(1)}, u32[]{:S(2)}, u32[]{:S(2)}) async-start(bf16[8,304,128]{2,1,0:T(8,128)(2,1)} %get-tuple-element.59), calls=%async_computation.5 | async-start | bytes 1245184 | tf_op jit(solution)/shard_map/all_to_all | solution.py:71
  99.0 2.7 %collective-permute-start.2 = (bf16[384,128]{1,0:T(8,128)(2,1)S(1)}, bf16[384,128]{1,0:T(8,128)(2,1)S(1)}, u32[]{:S(2)}, u32[]{:S(2)}) collective-permute-start(bf16[384,128]{1,0:T(8,128)(2,1)S(1)} %get-tuple-element.56), channel_id=1, source_target_pairs={{0,2},{1,7},{2,4},{3,1},{4,6},{5,3},{6,0},{7,5},{8,10},{9,15},{10,... | collective-permute-start | bytes 294920 | tf_op jit(solution)/shard_map/ppermute | solution.py:480
  101.7 5.3 %collective-permute-start.1 = (bf16[384,128]{1,0:T(8,128)(2,1)S(1)}, bf16[384,128]{1,0:T(8,128)(2,1)S(1)}, u32[]{:S(2)}, u32[]{:S(2)}) collective-permute-start(bf16[384,128]{1,0:T(8,128)(2,1)S(1)} %get-tuple-element.54), channel_id=1, source_target_pairs={{0,6},{1,3},{2,0},{3,5},{4,2},{5,7},{6,4},{7,1},{8,14},{9,11},{10,... | collective-permute-start | bytes 294920 | tf_op jit(solution)/shard_map/ppermute | solution.py:480
  106.9 3.6 %collective-permute-done.2.got_ref = bf16[384,128]{1,0:T(8,128)(2,1)S(1)} collective-permute-done((bf16[384,128]{1,0:T(8,128)(2,1)S(1)}, bf16[384,128]{1,0:T(8,128)(2,1)S(1)}, u32[]{:S(2)}, u32[]{:S(2)}) %collective-permute-start.2) | collective-permute-done | bytes 98336 | tf_op jit(solution)/shard_map/ppermute | solution.py:480
  110.5 1.9 %collective-permute-start.3 = (bf16[384,128]{1,0:T(8,128)(2,1)S(1)}, bf16[384,128]{1,0:T(8,128)(2,1)S(1)}, u32[]{:S(2)}, u32[]{:S(2)}) collective-permute-start(bf16[384,128]{1,0:T(8,128)(2,1)S(1)} %shard_map.138), channel_id=1, source_target_pairs={{0,2},{1,7},{2,4},{3,1},{4,6},{5,3},{6,0},{7,5},{8,10},{9,15},{10,... | collective-permute-start | bytes 294920 | tf_op jit(solution)/shard_map/ppermute | solution.py:480
  112.5 0.1 dynamic_slice.11
  112.6 0.0 collective-permute-done.1.refs_1_
  112.6 7.6 %collective-permute-done.3.refs_2_ = bf16[384,128]{1,0:T(8,128)(2,1)S(1)} collective-permute-done((bf16[384,128]{1,0:T(8,128)(2,1)S(1)}, bf16[384,128]{1,0:T(8,128)(2,1)S(1)}, u32[]{:S(2)}, u32[]{:S(2)}) %collective-permute-start.3) | collective-permute-done | bytes 98336 | tf_op jit(solution)/shard_map/ppermute | solution.py:480
  120.2 0.0 copy-done.2
  120.2 0.8 shard_map.139
  121.0 0.0 all-to-all-done.5.f_ref
  121.0 0.7 shard_map.142
  (4 shorter events, 0.1 us)
Async XLA Ops:
  0.6 30.6 %copy-start.3 = (bf16[128,128]{1,0:T(8,128)(2,1)S(1)}, bf16[128,128]{1,0:T(8,128)(2,1)}, u32[]{:S(2)}) copy-start(bf16[128,128]{1,0:T(8,128)(2,1)} %q_ref.1) | copy-start | bytes 98308
  32.3 5.9 %copy-start.6 = (s32[128]{0:T(128)S(1)}, s32[128]{0:T(128)}, u32[]{:S(2)}) copy-start(s32[128]{0:T(128)} %param.17) | copy-start | bytes 1540
  32.3 6.3 %copy-start.7 = (s32[128,128]{1,0:T(8,128)S(1)}, s32[128,128]{1,0:T(8,128)}, u32[]{:S(2)}) copy-start(s32[128,128]{1,0:T(8,128)} %param.16) | copy-start | bytes 196612
  32.3 6.8 %copy-start.4 = (bf16[128,3072]{1,0:T(8,128)(2,1)S(1)}, bf16[128,3072]{1,0:T(8,128)(2,1)}, u32[]{:S(2)}) copy-start(bf16[128,3072]{1,0:T(8,128)(2,1)} %param.15) | copy-start | bytes 2359300
  32.4 19.1 %all-to-all-start.1 = ((bf16[8,512,128]{2,1,0:T(8,128)(2,1)}), bf16[8,512,128]{2,1,0:T(8,128)(2,1)S(1)}, u32[]{:S(2)}, u32[]{:S(2)}) async-start(bf16[8,512,128]{2,1,0:T(8,128)(2,1)} %shard_map.129), calls=%async_computation.1 | async-start | bytes 2097152 | tf_op jit(solution)/shard_map/all_to_all | solution.py:71
  38.3 1.3 %copy-start.5 = (f32[3072]{0:T(1024)S(1)}, f32[3072]{0:T(1024)}, u32[]{:S(2)}) copy-start(f32[3072]{0:T(1024)} %param.13) | copy-start | bytes 36868
  53.0 10.7 %all-to-all-start.2 = ((bf16[8,128,128]{2,1,0:T(8,128)(2,1)}), bf16[8,128,128]{2,1,0:T(8,128)(2,1)S(1)}, u32[]{:S(2)}, u32[]{:S(2)}) async-start(bf16[8,128,128]{2,1,0:T(8,128)(2,1)} %shard_map.131), calls=%async_computation.2 | async-start | bytes 524288 | tf_op jit(solution)/shard_map/all_to_all | solution.py:71
  64.6 11.8 %all-to-all-start.3 = ((bf16[8,224,128]{2,1,0:T(8,128)(2,1)}), bf16[8,224,128]{2,1,0:T(8,128)(2,1)S(1)}, u32[]{:S(2)}, u32[]{:S(2)}) async-start(bf16[8,224,128]{2,1,0:T(8,128)(2,1)} %get-tuple-element.39), calls=%async_computation.3 | async-start | bytes 917504 | tf_op jit(solution)/shard_map/all_to_all | solution.py:71
  72.4 0.7 copy-start
  76.6 1.0 copy-start.1
  78.8 15.0 %all-to-all-start.4 = ((bf16[8,512,128]{2,1,0:T(8,128)(2,1)}), bf16[8,512,128]{2,1,0:T(8,128)(2,1)S(1)}, u32[]{:S(2)}, u32[]{:S(2)}) async-start(bf16[8,512,128]{2,1,0:T(8,128)(2,1)} %shard_map.135), calls=%async_computation.4 | async-start | bytes 2097152 | tf_op jit(solution)/shard_map/all_to_all | solution.py:71
  83.9 7.6 %collective-permute-start = (bf16[4,384,128]{2,1,0:T(8,128)(2,1)S(1)}, bf16[4,384,128]{2,1,0:T(8,128)(2,1)S(1)}, u32[]{:S(2)}, u32[]{:S(2)}) collective-permute-start(bf16[4,384,128]{2,1,0:T(8,128)(2,1)S(1)} %get-tuple-element.48), channel_id=1, source_target_pairs={{0,1},{1,0},{2,3},{3,2},{4,5},{5,4},{6,7},{7,6},{8,9},{9,8},{10,11... | collective-permute-start | bytes 1179656 | tf_op jit(solution)/shard_map/ppermute | solution.py:450
  95.3 24.9 %copy-start.2 = (bf16[128,384]{1,0:T(8,128)(2,1)S(1)}, bf16[128,384]{1,0:T(8,128)(2,1)}, u32[]{:S(2)}) copy-start(bf16[128,384]{1,0:T(8,128)(2,1)} %residual_ref.1) | copy-start | bytes 294916
  95.3 25.7 %all-to-all-start.5 = ((bf16[8,304,128]{2,1,0:T(8,128)(2,1)}), bf16[8,304,128]{2,1,0:T(8,128)(2,1)S(1)}, u32[]{:S(2)}, u32[]{:S(2)}) async-start(bf16[8,304,128]{2,1,0:T(8,128)(2,1)} %get-tuple-element.59), calls=%async_computation.5 | async-start | bytes 1245184 | tf_op jit(solution)/shard_map/all_to_all | solution.py:71
  99.0 11.5 %collective-permute-start.2 = (bf16[384,128]{1,0:T(8,128)(2,1)S(1)}, bf16[384,128]{1,0:T(8,128)(2,1)S(1)}, u32[]{:S(2)}, u32[]{:S(2)}) collective-permute-start(bf16[384,128]{1,0:T(8,128)(2,1)S(1)} %get-tuple-element.56), channel_id=1, source_target_pairs={{0,2},{1,7},{2,4},{3,1},{4,6},{5,3},{6,0},{7,5},{8,10},{9,15},{10,... | collective-permute-start | bytes 294920 | tf_op jit(solution)/shard_map/ppermute | solution.py:480
  101.7 10.9 %collective-permute-start.1 = (bf16[384,128]{1,0:T(8,128)(2,1)S(1)}, bf16[384,128]{1,0:T(8,128)(2,1)S(1)}, u32[]{:S(2)}, u32[]{:S(2)}) collective-permute-start(bf16[384,128]{1,0:T(8,128)(2,1)S(1)} %get-tuple-element.54), channel_id=1, source_target_pairs={{0,6},{1,3},{2,0},{3,5},{4,2},{5,7},{6,4},{7,1},{8,14},{9,11},{10,... | collective-permute-start | bytes 294920 | tf_op jit(solution)/shard_map/ppermute | solution.py:480
  110.5 9.7 %collective-permute-start.3 = (bf16[384,128]{1,0:T(8,128)(2,1)S(1)}, bf16[384,128]{1,0:T(8,128)(2,1)S(1)}, u32[]{:S(2)}, u32[]{:S(2)}) collective-permute-start(bf16[384,128]{1,0:T(8,128)(2,1)S(1)} %shard_map.138), channel_id=1, source_target_pairs={{0,2},{1,7},{2,4},{3,1},{4,6},{5,3},{6,0},{7,5},{8,10},{9,15},{10,... | collective-permute-start | bytes 294920 | tf_op jit(solution)/shard_map/ppermute | solution.py:480
